TPU v7x, 32 devices: a whole 2x2x4 slice. The times are simulated.
32 devices in a mesh: gz: 8 (over z, y), pa: 4 (over x, core).
Axes of the slice: x: 2, y: 2, z: 4, core: 2. Of those that a mesh axis runs over, the one named last changes fastest.
Arguments:
- velocity: float32 [3, 8, 192, 512], P(None, 'gz', None, 'pa'), may hold values from -4 to 4
- viscosity: float32 [8, 192, 512], P('gz', None, 'pa'), may hold values from 0.2 to 2
- parcels: float32 [32768, 16], P(('gz', 'pa')), may hold values from -4 to 4, as said below
- dest_rank: int32 [32768, 1], P(('gz', 'pa')), may hold values from 0 to 7; in each aligned block of 1024 rows (0 to 1023, 1024 to 2047, ...) at most 384 rows name the same one
- dest_cell: int32 [32768], P(('gz', 'pa')), may hold values from 0 to 24575
- counts: int32 [32], P(('gz', 'pa')), may hold values from 1 to 1024, 24576 in all
Outputs:
- velocity_out: float32 [3, 8, 192, 512], P(None, 'gz', None, 'pa')
- parcels_out: float32 [98304, 16], P(('gz', 'pa'))
Inputs may be any that keep to these rules, and one draw needn't show every extreme that they name: `dest_rank`: among the 1024 rows of one device no slab is named more than 384 times, and some block names one slab exactly 384 times. `counts`: some device has all 1024 rows live. `parcels`: columns 4 k + 3 hold positive drag rates.
All inputs are finite; a program needn't handle non-finite values.
Results may differ from a plain program's by a relative error of at most 0.0011.
Values sent between devices are 32-bit elements; how exact they have to be, the bound alone decides.
A program may use at most 64 MiB of HBM per device.

v0:
```python
import math

import jax
import jax.numpy as jnp
from jax import lax
from jax.sharding import PartitionSpec as P

NR = 192
NTH = 512


time_step = 0.1
shift_plane = 0.0001
highest = lax.Precision.HIGHEST


def padded_2(x, sides, width):
    for axis, dim in sides:
        count, length = (lax.axis_size(axis), x.shape[dim])
        up = [(i, (i + 1) % count) for i in range(count)]
        down = [(j, i) for i, j in up]
        last = lax.slice_in_dim(x, length - width, length, axis=dim)
        first = lax.slice_in_dim(x, 0, width, axis=dim)
        before = lax.ppermute(last, axis, up)
        after = lax.ppermute(first, axis, down)
        x = jnp.concatenate([before, x, after], axis=dim)
    return x


def radius_column(first, number):
    return (NR + first + jnp.arange(number) + 0.5).astype(jnp.float32)[:, None]


def viscous(extended, speeds, viscosity):
    planes, radii, columns = viscosity.shape
    radius = radius_column(0, radii)
    step_angle = 2.0 * math.pi / NTH
    arc_weight = 1.0 / (radius * step_angle) ** 2
    offsets = (
        (1, 0, 0, 1.0),
        (-1, 0, 0, 1.0),
        (0, 1, 0, (radius + 0.5) / radius),
        (0, -1, 0, (radius - 0.5) / radius),
        (0, 0, 1, arc_weight),
        (0, 0, -1, arc_weight),
    )
    total = jnp.zeros_like(speeds)
    for shift_z, shift_r, shift_t, weight in offsets:
        beside = extended[
            :,
            1 + shift_z : 1 + shift_z + planes,
            1 + shift_r : 1 + shift_r + radii,
            1 + shift_t : 1 + shift_t + columns,
        ]
        face_mean = 0.5 * (viscosity + beside[3])
        total = total + weight * face_mean * (beside[:3] - speeds)
    return total


def radial_divergence(radial_speed):
    radii = radial_speed.shape[-2]
    radius = radius_column(0, radii)
    mean_face = 0.5 * (radial_speed[..., 1:, :] + radial_speed[..., :-1, :])
    inner = (radius[1:] - 0.5) * mean_face
    zeros = jnp.zeros_like(radial_speed[..., :1, :])
    flux = jnp.concatenate([zeros, inner, zeros], axis=-2)
    return (flux[..., 1:, :] - flux[..., :-1, :]) / radius


def theta_difference(values, radius):
    step_angle = 2.0 * math.pi / NTH
    return (jnp.roll(values, -1, -1) - jnp.roll(values, 1, -1)) / (2.0 * step_angle * radius)


def radial_system(modes):
    radius = radius_column(0, NR)[:, 0]
    step_angle = 2.0 * math.pi / NTH
    arc_weight = 1.0 / (radius * step_angle) ** 2
    nothing = jnp.zeros((1,), jnp.float32)
    upper = jnp.concatenate([(radius[:-1] + 0.5) / radius[:-1], nothing])
    lower = jnp.concatenate([nothing, (radius[1:] - 0.5) / radius[1:]])
    spectrum = 2.0 - 2.0 * jnp.cos(step_angle * modes.astype(jnp.float32))
    diagonal = (
        shift_plane + arc_weight[None, :] * spectrum[:, None] + upper[None, :] + lower[None, :]
    )
    return (
        jnp.broadcast_to(-lower, diagonal.shape),
        diagonal,
        jnp.broadcast_to(-upper, diagonal.shape),
    )


def moved_along(values, stride, filler, axis, downward):
    length = values.shape[axis]
    filled = jnp.full_like(lax.slice_in_dim(values, 0, stride, axis=axis), filler)
    if downward:
        return jnp.concatenate(
            [filled, lax.slice_in_dim(values, 0, length - stride, axis=axis)], axis
        )
    return jnp.concatenate([lax.slice_in_dim(values, stride, length, axis=axis), filled], axis)


def reduce_cyclic(lower, diagonal, upper, right_side, axis):
    radii = right_side.shape[axis]
    padded_rows = 1
    while padded_rows < radii:
        padded_rows *= 2
    extra = padded_rows - radii
    widths = [(0, 0)] * right_side.ndim
    widths[axis] = (0, extra)
    lower = jnp.pad(lower, widths)
    upper = jnp.pad(upper, widths)
    diagonal = jnp.pad(diagonal, widths, constant_values=1.0)
    right_side = jnp.pad(right_side, widths)
    stride = 1
    while stride < padded_rows:
        ratio_low = lower / moved_along(diagonal, stride, 1.0, axis, True)
        ratio_high = upper / moved_along(diagonal, stride, 1.0, axis, False)
        new_diagonal = (
            diagonal
            - ratio_low * moved_along(upper, stride, 0.0, axis, True)
            - ratio_high * moved_along(lower, stride, 0.0, axis, False)
        )
        right_side = (
            right_side
            - ratio_low * moved_along(right_side, stride, 0.0, axis, True)
            - ratio_high * moved_along(right_side, stride, 0.0, axis, False)
        )
        lower = -ratio_low * moved_along(lower, stride, 0.0, axis, True)
        upper = -ratio_high * moved_along(upper, stride, 0.0, axis, False)
        diagonal = new_diagonal
        stride *= 2
    return lax.slice_in_dim(right_side / diagonal, 0, radii, axis=axis)


def mirror_gradient(values):
    padded = jnp.concatenate([values[..., :1, :], values, values[..., -1:, :]], axis=-2)
    return 0.5 * (padded[..., 2:, :] - padded[..., :-2, :])


def cas_table(waves, angles):
    product = waves[:, None] * angles[None, :] % NTH
    phase = 2.0 * math.pi / NTH * product.astype(jnp.float32)
    return jnp.cos(phase) + jnp.sin(phase)


def to_theta(values):
    return lax.all_to_all(values, "pa", split_axis=2, concat_axis=3, tiled=True)


def to_radial(values):
    return lax.all_to_all(values, "pa", split_axis=3, concat_axis=2, tiled=True)


def body(velocity, viscosity, parcels, dest_rank, dest_cell, counts):
    slabs = lax.axis_size("gz")
    planes, radii, columns = viscosity.shape
    block = parcels.shape[0]
    capacity = 3 * block // slabs
    cells_local = planes * radii * columns
    line_count = planes * radii
    live = jnp.arange(block) < counts[0]
    target = dest_rank[:, 0]
    marks = ((target[:, None] == jnp.arange(slabs)[None, :]) & live[:, None]).astype(jnp.int32)
    before = jnp.cumsum(marks, axis=0) - marks
    slot = jnp.sum(before * marks, axis=1)
    place = jnp.where(live, target * capacity + slot, slabs * capacity)
    outgoing = (
        jnp.zeros((slabs * capacity, 16), jnp.float32)
        .at[place]
        .set(parcels, mode="drop")
        .reshape(slabs, capacity, 16)
    )
    where_to = (
        jnp.full((slabs * capacity,), -1, jnp.int32)
        .at[place]
        .set(dest_cell, mode="drop")
        .reshape(slabs, capacity)
    )
    line_tables = velocity.reshape(3, line_count, columns)
    line_ids = jnp.arange(line_count)
    column_ids = jnp.arange(columns)
    rows = lax.all_to_all(outgoing, "gz", split_axis=0, concat_axis=0, tiled=True)
    cells = lax.all_to_all(where_to, "gz", split_axis=0, concat_axis=0, tiled=True)
    senders, count = cells.shape
    safe = jnp.clip(cells, 0, cells_local - 1).reshape(-1)
    line_hot = ((safe // columns)[:, None] == line_ids[None, :]).astype(jnp.float32)
    column_hot = ((safe % columns)[:, None] == column_ids[None, :]).astype(jnp.float32)
    looked = []
    for component in range(3):
        picked = jnp.dot(
            line_hot, line_tables[component], precision=highest, preferred_element_type=jnp.float32
        )
        looked.append(jnp.sum(picked * column_hot, axis=1))
    fluid = jnp.stack(looked, -1).reshape(senders, count, 3)
    classes = rows.reshape(senders, count, 4, 4)
    speed = classes[..., :3]
    rate = classes[..., 3:]
    moved = (speed + time_step * rate * fluid[:, :, None, :]) / (1.0 + time_step * rate)
    drag = jnp.sum(rate * (moved - fluid[:, :, None, :]), axis=2).astype(jnp.bfloat16)
    updated = jnp.concatenate([moved, rate], -1).reshape(rows.shape)
    arrived, drag, landed = (updated, drag, cells)
    parcels_out = arrived.reshape(slabs * capacity, 16)

    def deposit_step(carry, pair):
        cells, pushes = pair
        left = ((cells // columns)[:, None] == line_ids[None, :]).astype(jnp.bfloat16)
        column_hot = ((cells % columns)[:, None] == column_ids[None, :]).astype(jnp.bfloat16)
        added = []
        for component in range(3):
            right = pushes[:, component : component + 1] * column_hot
            added.append(
                lax.dot_general(
                    left, right, (((0,), (0,)), ((), ())), preferred_element_type=jnp.float32
                )
            )
        return (carry + jnp.stack(added), None)

    accum, _ = lax.scan(
        deposit_step,
        jnp.zeros((3, line_count, columns), jnp.float32),
        (landed.reshape(3, block), drag.reshape(3, block, 3)),
    )
    deposit = accum.reshape(3, planes, radii, columns)
    fields = jnp.concatenate([velocity, viscosity[None]], 0)
    bordered = padded_2(fields, (("gz", 1), ("pa", 3)), 1)
    slab_index = lax.axis_index("gz")
    lower_rim = jnp.where(slab_index > 0, bordered[:, :1], 0.0)
    upper_rim = jnp.where(slab_index < slabs - 1, bordered[:, -1:], 0.0)
    bordered = jnp.concatenate([lower_rim, bordered[:, 1:-1], upper_rim], 1)
    extended = jnp.pad(bordered, ((0, 0), (0, 0), (1, 1), (0, 0)))
    ustar = velocity + time_step * (viscous(extended, velocity, viscosity) + deposit)
    radial_part = radial_divergence(ustar[1])
    pencil_index = lax.axis_index("pa")
    radius = radius_column(0, NR)
    owned = pencil_index * columns + jnp.arange(columns)
    lower, diagonal, upper = radial_system(owned)
    theta_side = to_theta(jnp.stack([radial_part, ustar[2]]))
    band = theta_side.shape[2]
    band_radius = radius_column(pencil_index * band, band)
    table = cas_table(jnp.arange(NTH), jnp.arange(NTH))
    source = -(theta_side[0] + theta_difference(theta_side[1], band_radius))
    spectral = jnp.einsum("zrj,kj->zrk", source, table, precision=highest)
    spectral = to_radial(spectral[None])[0]
    correction = jnp.sum(radius * spectral, axis=1) / jnp.sum(radius)
    spectral = spectral - jnp.where((owned == 0)[None, None, :], correction[:, None, :], 0.0)
    potential_hat = reduce_cyclic(lower.T[None], diagonal.T[None], upper.T[None], spectral, 1)
    radial_hat = mirror_gradient(potential_hat)
    theta_side = to_theta(jnp.stack([radial_hat, potential_hat]))
    physical = jnp.einsum("fzrk,kj->fzrj", theta_side, table, precision=highest) / NTH
    gradients = to_radial(jnp.stack([physical[0], theta_difference(physical[1], band_radius)]))
    grad_r = gradients[0]
    grad_t = gradients[1]
    velocity_out = jnp.stack([ustar[0], ustar[1] - grad_r, ustar[2] - grad_t])
    return (velocity_out, parcels_out)


def solution(mesh):
    in_specs = (
        P(None, "gz", None, "pa"),
        P("gz", None, "pa"),
        P(("gz", "pa"), None),
        P(("gz", "pa"), None),
        P(("gz", "pa")),
        P(("gz", "pa")),
    )
    out_specs = (P(None, "gz", None, "pa"), P(("gz", "pa"), None))
    return jax.shard_map(body, mesh=mesh, in_specs=in_specs, out_specs=out_specs, check_vma=False)
```

profile of v0, /device:TPU:1, one launch (start us, length us, event | category | flops | bytes accessed | tf_op | source)
XLA Modules:
  0.0 129.8 jit_solution(18206935478111251707)
XLA Ops:
  1.7 5.2 %collective-permute-start.1 = (f32[4,1,192,128]{3,2,1,0:T(8,128)S(1)}, f32[4,1,192,128]{3,2,1,0:T(8,128)S(1)}, u32[]{:S(2)}, u32[]{:S(2)}) collective-permute-start(f32[4,1,192,128]{3,2,1,0:T(8,128)S(1)} %pad_maximum_fusion.2), channel_id=1, source_target_pairs={{4,0},{8,4},{12,8},{16,12},{20,16},{24,20},{28,24},{0,28},{5,1},{9... | collective-permute-start | bytes 1179656 | tf_op jit(solution)/shard_map/ppermute | solution.py:25
  8.2 2.3 %reduce-window.6 = s32[8,8,128]{2,1,0:T(8,128)S(1)} reduce-window(s32[8,8,128]{2,1,0:T(8,128)S(1)} %fusion.109, s32[]{:T(128)} %constant.178.clone.1), window={size=1x1x128 pad=0_0x0_0x127_0}, to_apply=%region_0.0 | reduce-window | flops 1040384 | bytes 65540 | tf_op jit(solution)/shard_map/reduce-window
  12.4 5.0 %scatter_custom_fusion = s32[3072]{0:T(1024)} fusion(s32[1024]{0:T(1024)S(1)} %bitcast.232, s32[1024]{0:T(1024)} %param.12, s32[]{:T(128)} %constant.182.clone.1), kind=kCustom, calls=%fused_computation.255 | custom fusion | bytes 12800 | tf_op jit(solution)/shard_map/scatter | solution.py:177
  17.5 5.4 %all-to-all-start = ((s32[8,1,384]{2,1,0:T(1,128)}), s32[8,1,384]{2,1,0:T(1,128)S(1)}, u32[]{:S(2)}, u32[]{:S(2)}) async-start(s32[8,1,384]{2,1,0:T(1,128)} %bitcast.19), calls=%async_computation | async-start | bytes 24576 | tf_op jit(solution)/shard_map/all_to_all | solution.py:184
  26.2 1.9 %copy.126 = f32[1024,16]{1,0:T(8,128)} copy(f32[1024,16]{0,1:T(8,128)} %param.10) | data formatting | bytes 131072 | tf_op args[2]
  28.1 3.9 %scatter_custom_fusion.1 = f32[3072,16]{1,0:T(8,128)S(1)} fusion(s32[1024]{0:T(1024)S(1)} %bitcast.233, f32[1024,16]{1,0:T(8,128)} %copy.126, f32[]{:T(128)} %constant.176.clone.1), kind=kCustom, calls=%fused_computation.73 | custom fusion | bytes 197120 | tf_op jit(solution)/shard_map/scatter | solution.py:171
  33.1 5.4 %all-to-all-start.1 = ((f32[8,384,16]{1,2,0:T(8,128)}), f32[8,384,16]{1,2,0:T(8,128)S(1)}, u32[]{:S(2)}, u32[]{:S(2)}) async-start(f32[8,384,16]{1,2,0:T(8,128)} %copy.127), calls=%async_computation.1 | async-start | bytes 393216 | tf_op jit(solution)/shard_map/all_to_all | solution.py:183
  38.6 2.6 %fusion.33 = f32[3072]{0:T(1024)S(1)} fusion(s32[3072]{0:T(1024)S(1)} %get-tuple-element.261, s32[3072]{0:T(1024)S(1)} %get-tuple-element.260, f32[3,1,192,128]{3,2,1,0:T(8,128)S(1)} %copy-done), kind=kOutput, calls=%fused_computation.60 | convolution fusion | flops 907736064 | bytes 135168 | tf_op jit(solution)/shard_map/dot_general | solution.py:191
  41.2 2.6 %fusion.31 = f32[3072]{0:T(1024)S(1)} fusion(s32[3072]{0:T(1024)S(1)} %get-tuple-element.261, s32[3072]{0:T(1024)S(1)} %get-tuple-element.260, f32[3,1,192,128]{3,2,1,0:T(8,128)S(1)} %copy-done), kind=kOutput, calls=%fused_computation.58 | convolution fusion | flops 907736064 | bytes 135168 | tf_op jit(solution)/shard_map/dot_general | solution.py:191
  43.8 2.6 %fusion.32 = f32[3072]{0:T(1024)S(1)} fusion(s32[3072]{0:T(1024)S(1)} %get-tuple-element.261, s32[3072]{0:T(1024)S(1)} %get-tuple-element.260, f32[3,1,192,128]{3,2,1,0:T(8,128)S(1)} %copy-done), kind=kOutput, calls=%fused_computation.59 | convolution fusion | flops 907736064 | bytes 135168 | tf_op jit(solution)/shard_map/dot_general | solution.py:191
  49.5 1.7 %copy.121 = f32[4,3,192,1]{2,0,3,1:T(4,128)S(1)} copy(f32[4,3,192,1]{3,2,1,0:T(8,128)} %get-tuple-element.168) | data formatting | bytes 18432 | tf_op jit(solution)/shard_map/slice | solution.py:23
  51.7 3.2 %collective-permute-start.2 = (f32[4,3,192,1]{2,0,3,1:T(4,128)S(1)}, f32[4,3,192,1]{2,0,3,1:T(4,128)S(1)}, u32[]{:S(2)}, u32[]{:S(2)}) collective-permute-start(f32[4,3,192,1]{2,0,3,1:T(4,128)S(1)} %copy.120), channel_id=1, source_target_pairs={{0,1},{1,2},{2,3},{3,0},{4,5},{5,6},{6,7},{7,4},{8,9},{9,10},{10,1... | collective-permute-start | bytes 27656 | tf_op jit(solution)/shard_map/ppermute | solution.py:24
  54.9 8.5 %while.13 = (s32[]{:T(128)}, f32[3,192,128]{2,1,0:T(8,128)S(1)}, s32[3,1024]{1,0:T(4,128)S(1)}, bf16[3,1024,3]{1,2,0:T(4,128)(2,1)S(1)}, s32[]{:T(128)}, /*index=5*/s32[]{:T(128)}) while((s32[]{:T(128)}, f32[3,192,128]{2,1,0:T(8,128)S(1)}, s32[3,1024]{1,0:T(4,128)S(1)}, bf16[3,1024,3]{1,2,0:T(4,128)(2,1)S(1)}, s32[]{:T(128)}, ...), condition=%wide.region_10.11_spmd.clone, body=%wide.region_9.10_spmd.clone.sunk | while | flops 152685568 | bytes 1255519 | solution.py:219
  64.3 2.0 %pad_maximum_fusion = f32[4,3,192,130]{3,2,1,0:T(8,128)S(1)} fusion(f32[4,3,192,1]{3,2,1,0:T(8,128)S(1)} %copy.123, f32[4,1,192,128]{3,2,1,0:T(8,128)S(1)} %collective-permute-done.1, f32[1,1,192,128]{3,2,1,0:T(8,128)S(1)} %bitcast.209, f32[3,1,192,128]{3,2,1,0:T(8,128)S(1)} %copy-done, f32[4,1,192,128]{3,2,1,0:T(8,128)} %copy-done.1, ...), kind=kLoop, calls=%fused_computation.50 | loop fusion | flops 1497600 | bytes 2396160 | tf_op jit(solution)/shard_map/concatenate | solution.py:26
  70.3 4.0 %all-to-all-start.2 = ((f32[2,1,192,128]{3,0,1,2:T(2,128)}), f32[2,1,192,128]{3,0,1,2:T(2,128)S(1)}, u32[]{:S(2)}, u32[]{:S(2)}) async-start(f32[2,1,192,128]{3,0,1,2:T(2,128)} %copy.130), calls=%async_computation.2 | async-start | bytes 393216 | tf_op jit(solution)/shard_map/all_to_all | solution.py:148
  75.2 3.5 %all-to-all-done.2 = f32[2,1,192,128]{3,0,1,2:T(2,128)S(1)} async-done(((f32[2,1,192,128]{3,0,1,2:T(2,128)}), f32[2,1,192,128]{3,0,1,2:T(2,128)S(1)}, u32[]{:S(2)}, u32[]{:S(2)}) %all-to-all-start.2) | async-done | bytes 196640 | tf_op jit(solution)/shard_map/all_to_all | solution.py:148
  79.2 5.0 %fusion.43 = f32[48,512]{0,1:T(8,128)S(1)} fusion(f32[6,8,4,128]{3,2,1,0:T(4,128)S(1)} %bitcast.226, f32[48,1]{1,0:T(8,128)S(1)} %get-tuple-element.253, f32[48,511]{1,0:T(8,128)S(1)} %get-tuple-element.255, f32[48,511]{1,0:T(8,128)S(1)} %get-tuple-element.254, f32[48,1]{1,0:T(8,128)S(1)} %get-tuple-element.252, f32[48]{0:T(128)S(1)} %add_multiply_fusion.1), kind=kOutput, calls=%fused_computation.75 | convolution fusion | flops 155074560 | bytes 393408 | tf_op jit(solution)/shard_map/zrj,kj->zrk/dot_general | solution.py:243
  86.9 4.4 %all-to-all-start.3 = ((f32[4,1,6144]{2,1,0:T(1,128)}), f32[4,1,6144]{2,1,0:T(1,128)S(1)}, u32[]{:S(2)}, u32[]{:S(2)}) async-start(f32[4,1,6144]{2,1,0:T(1,128)} %reshape.614), calls=%async_computation.3 | async-start | bytes 196608 | tf_op jit(solution)/shard_map/all_to_all | solution.py:152
  91.3 3.3 %all-to-all-done.3 = f32[4,1,6144]{2,1,0:T(1,128)S(1)} async-done(((f32[4,1,6144]{2,1,0:T(1,128)}), f32[4,1,6144]{2,1,0:T(1,128)S(1)}, u32[]{:S(2)}, u32[]{:S(2)}) %all-to-all-start.3) | async-done | bytes 98336 | tf_op jit(solution)/shard_map/all_to_all | solution.py:152
  99.6 7.9 %all_to_all.74 = f32[2,1,192,128]{3,1,0,2:T(1,128)S(1)} all-to-all(f32[2,1,192,128]{3,1,0,2:T(1,128)S(1)} %copy.138), channel_id=1, replica_groups=mesh['gz'=8,'pa'=4] {'pa'}, dimensions={2} | all-to-all | bytes 393216 | tf_op jit(solution)/shard_map/all_to_all | solution.py:148
  107.7 5.1 %convolution_multiply_fusion = f32[2,48,512]{2,1,0:T(8,128)S(1)} fusion(f32[2,48,512]{2,1,0:T(8,128)S(1)} %reshape.587), kind=kOutput, calls=%fused_computation.62 | convolution fusion | flops 305971200 | bytes 393216 | tf_op jit(solution)/shard_map/fzrk,kj->fzrj/dot_general | solution.py:250
  113.5 2.4 %reduce.14 = f32[512,2,48]{2,1,0:T(2,128)S(1)} reduce(f32[512,2,1,48]{3,2,1,0:T(1,128)S(1)} %bitcast.212, f32[]{:T(128)} %broadcast.809), dimensions={2}, to_apply=%bitcast.186.reduce_sub_computation | reduce | bytes 393220
  117.5 4.1 %all-to-all-start.5 = ((f32[4,1,12288]{2,1,0:T(1,128)}), f32[4,1,12288]{2,1,0:T(1,128)S(1)}, u32[]{:S(2)}, u32[]{:S(2)}) async-start(f32[4,1,12288]{2,1,0:T(1,128)} %reshape.616), calls=%async_computation.5 | async-start | bytes 393216 | tf_op jit(solution)/shard_map/all_to_all | solution.py:152
  122.4 3.7 %all-to-all-done.5 = f32[4,1,12288]{2,1,0:T(1,128)S(1)} async-done(((f32[4,1,12288]{2,1,0:T(1,128)}), f32[4,1,12288]{2,1,0:T(1,128)S(1)}, u32[]{:S(2)}, u32[]{:S(2)}) %all-to-all-start.5) | async-done | bytes 196640 | tf_op jit(solution)/shard_map/all_to_all | solution.py:152
  (199 shorter events, 40.2 us)
Async XLA Ops:
  1.7 46.3 %collective-permute-start.1 = (f32[4,1,192,128]{3,2,1,0:T(8,128)S(1)}, f32[4,1,192,128]{3,2,1,0:T(8,128)S(1)}, u32[]{:S(2)}, u32[]{:S(2)}) collective-permute-start(f32[4,1,192,128]{3,2,1,0:T(8,128)S(1)} %pad_maximum_fusion.2), channel_id=1, source_target_pairs={{4,0},{8,4},{12,8},{16,12},{20,16},{24,20},{28,24},{0,28},{5,1},{9... | collective-permute-start | bytes 1179656 | tf_op jit(solution)/shard_map/ppermute | solution.py:25
  6.8 41.1 %collective-permute-start = (f32[4,1,192,128]{3,2,1,0:T(8,128)S(1)}, f32[4,1,192,128]{3,2,1,0:T(8,128)S(1)}, u32[]{:S(2)}, u32[]{:S(2)}) collective-permute-start(f32[4,1,192,128]{3,2,1,0:T(8,128)S(1)} %pad_maximum_fusion.2), channel_id=1, source_target_pairs={{0,4},{4,8},{8,12},{12,16},{16,20},{20,24},{24,28},{28,0},{1,5},{5... | collective-permute-start | bytes 1179656 | tf_op jit(solution)/shard_map/ppermute | solution.py:24
  17.5 15.6 %all-to-all-start = ((s32[8,1,384]{2,1,0:T(1,128)}), s32[8,1,384]{2,1,0:T(1,128)S(1)}, u32[]{:S(2)}, u32[]{:S(2)}) async-start(s32[8,1,384]{2,1,0:T(1,128)} %bitcast.19), calls=%async_computation | async-start | bytes 24576 | tf_op jit(solution)/shard_map/all_to_all | solution.py:184
  28.1 10.5 %copy-start = (f32[3,1,192,128]{3,2,1,0:T(8,128)S(1)}, f32[3,1,192,128]{3,2,1,0:T(8,128)}, u32[]{:S(2)}) copy-start(f32[3,1,192,128]{3,2,1,0:T(8,128)} %param.8) | copy-start | bytes 884740
  33.1 13.4 %all-to-all-start.1 = ((f32[8,384,16]{1,2,0:T(8,128)}), f32[8,384,16]{1,2,0:T(8,128)S(1)}, u32[]{:S(2)}, u32[]{:S(2)}) async-start(f32[8,384,16]{1,2,0:T(8,128)} %copy.127), calls=%async_computation.1 | async-start | bytes 393216 | tf_op jit(solution)/shard_map/all_to_all | solution.py:183
  43.8 4.1 %copy-start.3 = (f32[1,192,128]{2,1,0:T(8,128)S(1)}, f32[1,192,128]{2,1,0:T(8,128)}, u32[]{:S(2)}) copy-start(f32[1,192,128]{2,1,0:T(8,128)} %param.9) | copy-start | bytes 294916
  48.0 1.5 %copy-start.1 = (f32[4,1,192,128]{3,2,1,0:T(8,128)}, f32[4,1,192,128]{3,2,1,0:T(8,128)S(1)}, u32[]{:S(2)}) copy-start(f32[4,1,192,128]{3,2,1,0:T(8,128)S(1)} %collective-permute-done) | copy-start | bytes 1179652
  51.7 12.2 %collective-permute-start.2 = (f32[4,3,192,1]{2,0,3,1:T(4,128)S(1)}, f32[4,3,192,1]{2,0,3,1:T(4,128)S(1)}, u32[]{:S(2)}, u32[]{:S(2)}) collective-permute-start(f32[4,3,192,1]{2,0,3,1:T(4,128)S(1)} %copy.120), channel_id=1, source_target_pairs={{0,1},{1,2},{2,3},{3,0},{4,5},{5,6},{6,7},{7,4},{8,9},{9,10},{10,1... | collective-permute-start | bytes 27656 | tf_op jit(solution)/shard_map/ppermute | solution.py:24
  54.9 8.5 %collective-permute-start.3 = (f32[4,3,192,1]{2,0,3,1:T(4,128)S(1)}, f32[4,3,192,1]{2,0,3,1:T(4,128)S(1)}, u32[]{:S(2)}, u32[]{:S(2)}) collective-permute-start(f32[4,3,192,1]{2,0,3,1:T(4,128)S(1)} %copy.121), channel_id=1, source_target_pairs={{1,0},{2,1},{3,2},{0,3},{5,4},{6,5},{7,6},{4,7},{9,8},{10,9},{11,1... | collective-permute-start | bytes 27656 | tf_op jit(solution)/shard_map/ppermute | solution.py:25
  66.5 1.0 copy-start.2
  66.5 1.0 copy-start.11
  66.5 1.0 copy-start.12
  66.5 1.0 copy-start.13
  67.8 1.4 %copy-start.10 = (f32[191]{0:T(256)S(1)}, f32[191]{0:T(256)}, u32[]{:S(2)}) copy-start(f32[191]{0:T(256)} %get-tuple-element.273) | copy-start | bytes 2296
  68.5 0.7 copy-start.4
  69.2 5.1 %copy-start.8 = (f32[192]{0:T(256)S(1)}, f32[192]{0:T(256)}, u32[]{:S(2)}) copy-start(f32[192]{0:T(256)} %get-tuple-element.268) | copy-start | bytes 2308
  69.2 5.1 %copy-start.9 = (f32[192]{0:T(256)S(1)}, f32[192]{0:T(256)}, u32[]{:S(2)}) copy-start(f32[192]{0:T(256)} %get-tuple-element.270) | copy-start | bytes 2308
  70.3 8.4 %all-to-all-start.2 = ((f32[2,1,192,128]{3,0,1,2:T(2,128)}), f32[2,1,192,128]{3,0,1,2:T(2,128)S(1)}, u32[]{:S(2)}, u32[]{:S(2)}) async-start(f32[2,1,192,128]{3,0,1,2:T(2,128)} %copy.130), calls=%async_computation.2 | async-start | bytes 393216 | tf_op jit(solution)/shard_map/all_to_all | solution.py:148
  86.9 7.7 %all-to-all-start.3 = ((f32[4,1,6144]{2,1,0:T(1,128)}), f32[4,1,6144]{2,1,0:T(1,128)S(1)}, u32[]{:S(2)}, u32[]{:S(2)}) async-start(f32[4,1,6144]{2,1,0:T(1,128)} %reshape.614), calls=%async_computation.3 | async-start | bytes 196608 | tf_op jit(solution)/shard_map/all_to_all | solution.py:152
  113.1 8.5 %copy-start.6 = (f32[8,384,4,3]{1,0,3,2:T(8,128)S(1)}, f32[8,384,4,3]{1,0,3,2:T(8,128)}, u32[]{:S(2)}) copy-start(f32[8,384,4,3]{1,0,3,2:T(8,128)} %get-tuple-element.158) | copy-start | bytes 442372
  113.1 8.5 %copy-start.7 = (f32[8,384,4,1]{1,0,3,2:T(8,128)S(1)}, f32[8,384,4,1]{1,0,3,2:T(8,128)}, u32[]{:S(2)}) copy-start(f32[8,384,4,1]{1,0,3,2:T(8,128)} %get-tuple-element.180) | copy-start | bytes 147460
  117.5 8.5 %all-to-all-start.5 = ((f32[4,1,12288]{2,1,0:T(1,128)}), f32[4,1,12288]{2,1,0:T(1,128)S(1)}, u32[]{:S(2)}, u32[]{:S(2)}) async-start(f32[4,1,12288]{2,1,0:T(1,128)} %reshape.616), calls=%async_computation.5 | async-start | bytes 393216 | tf_op jit(solution)/shard_map/all_to_all | solution.py:152
  121.6 7.4 %copy-start.5 = (f32[3,1,192,128]{3,2,1,0:T(8,128)S(1)}, f32[3,1,192,128]{3,2,1,0:T(8,128)}, u32[]{:S(2)}) copy-start(f32[3,1,192,128]{3,2,1,0:T(8,128)} %copy-done.4) | copy-start | bytes 884740
where the time goes:
time: 132 us; the launch traced here: 130 us
  starting transfers between devices  31.7 us (24%)
  local copies, waits for them, and re-layouts  27.5 us (21%)
  matrix products  25.7 us (19%)
  other arithmetic  24 us (18%)
  waiting for transfers between devices  10.6 us (8%)
  blocking collectives  7.91 us (6%)
  between operations  2.22 us (2%)
    unnamed x36, local copies, waits for them, and re-layouts  8.61 us
    all_to_all x2, starting transfers between devices, to_radial(): return lax.all_to_all(values, 'pa', split_axis=3, concat_axis=2, tiled=True)  8.44 us
    all_to_all x1, blocking collectives, to_theta(): return lax.all_to_all(values, 'pa', split_axis=2, concat_axis=3, tiled=True)  7.91 us
    dot_general x9, matrix products, deposit_step(): lax.dot_general(left, right, (((0,), (0,)), ((), ())), preferred_element_...  7.86 us
    dot_general x3, matrix products, body(): jnp.dot(line_hot, line_tables[component], precision=highest, preferred_el...  7.81 us
    all_to_all x2, waiting for transfers between devices, to_radial(): return lax.all_to_all(values, 'pa', split_axis=3, concat_axis=2, tiled=True)  7.04 us
    all_to_all x1, starting transfers between devices, body(): lax.all_to_all(outgoing, 'gz', split_axis=0, concat_axis=0, tiled=True)  5.44 us
    all_to_all x1, starting transfers between devices, body(): lax.all_to_all(where_to, 'gz', split_axis=0, concat_axis=0, tiled=True)  5.44 us
  transfers between devices with their start and end apart: 9, of which 3 were waited for; matrix products, arithmetic and copies ran while one was open for 31% of the time, Pallas kernels for 0%

commit v1 on v0

v1 whole, which is shorter than its diff:
```python
import functools
import math

import jax
import jax.numpy as jnp
import ml_dtypes
import numpy as np
from jax import lax
from jax.experimental import pallas as pl
from jax.experimental.pallas import tpu as pltpu
from jax.sharding import PartitionSpec as P

NR = 192
NTH = 512
STEP = 0.1
SHIFT = 0.0001
LIMIT = 48 * 1024 * 1024
MESH = pl.DeviceIdType.MESH
f32 = jnp.float32
bf16 = jnp.bfloat16
VM = pl.BlockSpec(memory_space=pltpu.VMEM)


def cas(n):
    x = 2.0 * np.pi / NTH * (n % NTH)
    return np.cos(x) + np.sin(x)


def halves(table):
    high = table.astype(np.float32).astype(ml_dtypes.bfloat16)
    low = (table - high.astype(np.float64)).astype(np.float32).astype(ml_dtypes.bfloat16)
    return high, low


@functools.lru_cache(None)
def forward_table(pa):
    columns = NTH // pa
    k = np.arange(NTH)[None, :]
    j = np.arange(NTH)[:, None]
    same = -cas(k * j)
    beside = -(cas(k * (j - 1)) - cas(k * (j + 1)))
    both = [np.concatenate([same[p * columns:(p + 1) * columns], beside[p * columns:(p + 1) * columns]], 0) for p in range(pa)]
    return halves(np.stack(both))


@functools.lru_cache(None)
def inverse_table(pa):
    columns = NTH // pa
    k = np.arange(NTH)[:, None]
    j = np.arange(NTH)[None, :]
    same = cas(k * j) / NTH
    beside = (cas(k * (j + 1)) - cas(k * (j - 1))) / NTH
    parts = []
    for p in range(pa):
        part = slice(p * columns, (p + 1) * columns)
        parts.append(np.stack([same[:, part], beside[:, part]]))
    return halves(np.stack(parts))


@functools.lru_cache(None)
def radial_ratios(pa):
    radius = NR + np.arange(NR) + 0.5
    step = 2.0 * np.pi / NTH
    arc = 1.0 / (radius * step) ** 2
    up = (radius + 0.5) / radius
    down = (radius - 0.5) / radius
    up[-1] = 0.0
    down[0] = 0.0
    k = np.arange(NTH)
    diagonal = SHIFT + arc[:, None] * (2.0 - 2.0 * np.cos(step * k))[None, :] + up[:, None] + down[:, None]
    lower = np.broadcast_to(-down[:, None], diagonal.shape)
    upper = np.broadcast_to(-up[:, None], diagonal.shape)

    def moved(x, s, fill):
        pad = np.full((abs(s), NTH), fill)
        return np.concatenate([pad, x[:-s]], 0) if s > 0 else np.concatenate([x[-s:], pad], 0)

    out = []
    stride = 1
    while stride < NR:
        low = lower / moved(diagonal, stride, 1.0)
        high = upper / moved(diagonal, -stride, 1.0)
        out += [low, high]
        diagonal = diagonal - low * moved(upper, stride, 0.0) - high * moved(lower, -stride, 0.0)
        lower = -low * moved(lower, stride, 0.0)
        upper = -high * moved(upper, -stride, 0.0)
        stride *= 2
    out.append(1.0 / diagonal)
    whole = np.stack(out).astype(np.float32)
    columns = NTH // pa
    return np.stack([whole[:, :, p * columns:(p + 1) * columns] for p in range(pa)])


def iota(shape, axis):
    return lax.broadcasted_iota(jnp.int32, shape, axis)


def radii():
    return (iota((NR, 1), 0) + NR).astype(f32) + 0.5


def rolled(x, s):
    return jnp.concatenate([x[s:], x[:s]], 0)


def rates_of(x):
    is_rate = iota(x.shape, 0) % 4 == 3
    w = jnp.where(is_rate, x, 0.0)
    return is_rate, w + rolled(w, 1) + rolled(w, 2) + rolled(w, 3)


def pack_kernel(gz, capacity, counts, rank, cell, parcels, first, second):
    block = rank.shape[1]
    tiles = capacity // 128
    live = iota((1, block), 1) < counts[0]
    target = jnp.where(live, rank[...], gz)
    marks = (iota((gz, block), 0) == target).astype(f32)
    earlier = (iota((128, 128), 0) < iota((128, 128), 1)).astype(f32).astype(bf16)
    carry = jnp.zeros((gz, 1), f32)
    slots = []
    for b in range(block // 128):
        part = marks[:, 128 * b:128 * b + 128]
        before = jnp.dot(part.astype(bf16), earlier, preferred_element_type=f32) + carry
        slots.append(jnp.sum(before * part, axis=0, keepdims=True))
        carry = carry + jnp.sum(part, axis=1, keepdims=True)
    slot = jnp.concatenate(slots, 1).astype(jnp.int32)
    place = jnp.where(live, target * capacity + slot, -1)
    high = place >> 7
    low = place & 127
    low_hot = (iota((128, block), 0) == low).astype(f32).astype(bf16)
    values = parcels[...]
    one = values.astype(bf16).astype(f32)
    two = (values - one).astype(bf16).astype(f32)
    three = values - one - two
    cells = cell[...]
    line = ((cells >> 7) + 1).astype(f32)
    column = (cells & 127).astype(f32)
    table = jnp.concatenate([one, two, three, line, column, jnp.zeros((14, block), f32)], 0)

    def slab(g, _):
        left = [jnp.where(high == g * tiles + i, table, 0.0).astype(bf16) for i in range(tiles)]
        got = lax.dot_general(jnp.concatenate(left, 0), low_hot, (((1,), (1,)), ((), ())), preferred_element_type=f32)
        for i in range(tiles):
            r = got[64 * i:64 * i + 64]
            rows = r[0:16] + r[16:32] + r[32:48]
            lanes = slice(128 * i, 128 * i + 128)
            second[g, :, lanes] = rows
            code = r[48:49] * 128.0 + r[49:50]
            total = 0.0
            for half in (rows[0:8], rows[8:16]):
                is_rate, rate = rates_of(half)
                weight = rate / (1.0 + STEP * rate)
                total = total + jnp.where(is_rate, weight, weight * half)
            total = total + rolled(total, 4)
            first[g, :, lanes] = jnp.where(iota(total.shape, 0) == 4, code, total)
        return 0

    lax.fori_loop(0, gz, slab, 0, unroll=gz <= 8)


def loop(first, last, step):
    if last - first <= 8:
        for i in range(first, last):
            step(i)
    else:
        lax.fori_loop(first, last, lambda i, _: (step(i), 0)[1], 0)


def route_kernel(gz, pa, first, edges, first_out, left_out, right_out, send, recv, esend, erecv):
    me = lax.axis_index("gz")
    mp = lax.axis_index("pa")
    right = lax.rem(mp + 1, pa)
    left = lax.rem(mp + pa - 1, pa)
    barrier = pltpu.get_barrier_semaphore()

    def greet(o):
        pl.semaphore_signal(barrier, inc=1, device_id=(lax.rem(me + o, gz), mp), device_id_type=MESH)

    loop(1, gz, greet)
    for q in (left, right):
        pl.semaphore_signal(barrier, inc=1, device_id=(me, q), device_id_type=MESH)
    pl.semaphore_wait(barrier, gz + 1)

    def copy(o):
        to = lax.rem(me + o, gz)
        return pltpu.make_async_remote_copy(
            src_ref=first.at[to], dst_ref=first_out.at[me], send_sem=send.at[o], recv_sem=recv.at[o],
            device_id=(to, mp), device_id_type=MESH)

    to_right = pltpu.make_async_remote_copy(
        src_ref=edges, dst_ref=left_out, send_sem=esend.at[0], recv_sem=erecv.at[0],
        device_id=(me, right), device_id_type=MESH)
    to_left = pltpu.make_async_remote_copy(
        src_ref=edges, dst_ref=right_out, send_sem=esend.at[1], recv_sem=erecv.at[1],
        device_id=(me, left), device_id_type=MESH)
    loop(1, gz, lambda o: copy(o).start())
    to_right.start()
    to_left.start()
    first_out[me] = first[me]
    loop(1, gz, lambda o: copy(o).wait())
    to_right.wait()
    to_left.wait()


def deposit_kernel(gz, first, velocity, fluid, deposit):
    columns = velocity.shape[2]
    capacity = first.shape[2]
    pieces = []
    for c in range(3):
        turned = velocity[c].T
        top = turned.astype(bf16)
        pieces += [top, (turned - top.astype(f32)).astype(bf16)]
    turned = jnp.concatenate(pieces, 0)
    deposit[...] = jnp.zeros_like(deposit)

    def slab(g, _):
        rows = first[g]
        code = rows[4:5].astype(jnp.int32)
        line = (code >> 7) - 1
        column = code & 127
        line_hot = (iota((NR, capacity), 0) == line).astype(f32).astype(bf16)
        column_hot = iota((columns, capacity), 0) == column
        picked = jnp.dot(turned, line_hot, preferred_element_type=f32)
        looked, pushes = [], []
        for c in range(3):
            both = picked[2 * c * columns:(2 * c + 1) * columns] + picked[(2 * c + 1) * columns:(2 * c + 2) * columns]
            speed = jnp.sum(jnp.where(column_hot, both, 0.0), axis=0, keepdims=True)
            drag = (rows[c:c + 1] - speed * rows[3:4]).astype(bf16).astype(f32)
            looked.append(speed)
            pushes.append(jnp.where(column_hot, drag, 0.0).astype(bf16))
        nothing = jnp.zeros_like(looked[0])
        fluid[g] = jnp.concatenate((looked + [nothing]) * 2, 0)
        added = lax.dot_general(line_hot, jnp.concatenate(pushes, 0), (((1,), (1,)), ((), ())), preferred_element_type=f32)
        for c in range(3):
            deposit[c] += added[:, c * columns:(c + 1) * columns]
        return 0

    lax.fori_loop(0, gz, slab, 0, unroll=gz <= 8)


def split_dot(x, high, low):
    top = x.astype(bf16)
    rest = (x - top.astype(f32)).astype(bf16)
    out = jnp.dot(top, low, preferred_element_type=f32) + jnp.dot(rest, high, preferred_element_type=f32)
    return out + jnp.dot(top, high, preferred_element_type=f32)


def momentum_kernel(pa, where, velocity, viscosity, above, below, edge_left, edge_right, deposit, high, low, ustar, partial):
    columns = velocity.shape[2]
    radius = radii()
    arc = 1.0 / (radius * (2.0 * math.pi / NTH)) ** 2
    nu = viscosity[...]
    row = iota((NR, columns), 0)
    lane = iota((NR, columns), 1)

    def outward(x):
        return jnp.concatenate([x[1:], jnp.zeros_like(x[:1])], 0)

    def inward(x):
        return jnp.concatenate([jnp.zeros_like(x[:1]), x[:-1]], 0)

    def ahead(x, f):
        return jnp.where(lane == columns - 1, edge_right[:, f:f + 1], pltpu.roll(x, columns - 1, 1))

    def behind(x, f):
        return jnp.where(lane == 0, edge_left[:, 4 + f:5 + f], pltpu.roll(x, 1, 1))

    weights = [
        0.5 * (nu + above[3]),
        0.5 * (nu + below[3]),
        (radius + 0.5) / radius * 0.5 * (nu + outward(nu)),
        (radius - 0.5) / radius * 0.5 * (nu + inward(nu)),
        arc * 0.5 * (nu + ahead(nu, 3)),
        arc * 0.5 * (nu + behind(nu, 3)),
    ]
    new = []
    for c in range(3):
        u = velocity[c]
        sides = (above[c], below[c], outward(u), inward(u), ahead(u, c), behind(u, c))
        total = weights[0] * (sides[0] - u)
        for w, s in zip(weights[1:], sides[1:]):
            total = total + w * (s - u)
        new.append(u + STEP * (total + deposit[c]))
        ustar[c] = new[c]
    radial = new[1]
    flux = jnp.where(row == NR - 1, 0.0, (radius + 0.5) * 0.5 * (radial + outward(radial)))
    divergence = (flux - inward(flux)) / radius
    across = new[2] / (2.0 * (2.0 * math.pi / NTH) * radius)
    out = split_dot(jnp.concatenate([divergence, across], 1), high[0], low[0])
    for q in range(pa):
        partial[q] = out[:, q * columns:(q + 1) * columns]


def solve_kernel(gz, pa, second, partial, ratios, second_out, hat, came, held, send, recv, rsend, rrecv, gsend, grecv, lsem):
    me = lax.axis_index("gz")
    mp = lax.axis_index("pa")
    columns = partial.shape[2]
    load = pltpu.make_async_copy(ratios.at[mp], held, lsem)
    load.start()
    barrier = pltpu.get_barrier_semaphore()

    def greet(o):
        pl.semaphore_signal(barrier, inc=1, device_id=(lax.rem(me + o, gz), mp), device_id_type=MESH)

    loop(1, gz, greet)
    others = [lax.rem(mp + o, pa) for o in range(1, pa)]
    for q in others:
        pl.semaphore_signal(barrier, inc=1, device_id=(me, q), device_id_type=MESH)
    pl.semaphore_wait(barrier, gz + pa - 2)

    sums = [
        pltpu.make_async_remote_copy(
            src_ref=partial.at[q], dst_ref=came.at[i], send_sem=rsend.at[i], recv_sem=rrecv.at[i],
            device_id=(me, q), device_id_type=MESH)
        for i, q in enumerate(others)
    ]
    for c in sums:
        c.start()

    def copy(o):
        to = lax.rem(me + o, gz)
        return pltpu.make_async_remote_copy(
            src_ref=second.at[to], dst_ref=second_out.at[me], send_sem=send.at[o], recv_sem=recv.at[o],
            device_id=(to, mp), device_id_type=MESH)

    loop(1, gz, lambda o: copy(o).start())
    second_out[me] = second[me]
    load.wait()
    for c in sums:
        c.wait()
    x = partial[mp]
    for i in range(pa - 1):
        x = x + came[i]
    radius = radii()
    mean = jnp.sum(radius * x, axis=0, keepdims=True) * (1.0 / (NR * (NR + NR / 2)))
    x = x - jnp.where(iota((1, columns), 1) + mp * columns == 0, mean, 0.0)
    stride, n = 1, 0
    while stride < NR:
        pad = jnp.zeros((stride, columns), f32)
        lower = jnp.concatenate([pad, x[:-stride]], 0)
        upper = jnp.concatenate([x[stride:], pad], 0)
        x = x - held[n] * lower - held[n + 1] * upper
        stride, n = stride * 2, n + 2
    hat[mp] = x * held[n]
    spread = [
        pltpu.make_async_remote_copy(
            src_ref=hat.at[mp], dst_ref=hat.at[mp], send_sem=gsend.at[i], recv_sem=grecv.at[i],
            device_id=(me, q), device_id_type=MESH)
        for i, q in enumerate(others)
    ]
    for c in spread:
        c.start()
    for c in spread:
        c.wait()
    loop(1, gz, lambda o: copy(o).wait())


def finish_kernel(gz, pa, flat, where, hat, ustar, high, low, second, fluid, velocity_out, parcels_out):
    capacity = second.shape[2]
    x = jnp.concatenate([hat[q] for q in range(pa)], 1)
    slope = 0.5 * (jnp.concatenate([x[1:], x[-1:]], 0) - jnp.concatenate([x[:1], x[:-1]], 0))
    velocity_out[0] = ustar[0]
    velocity_out[1] = ustar[1] - split_dot(slope, high[0, 0], low[0, 0])
    turn = split_dot(x, high[0, 1], low[0, 1]) / (2.0 * (2.0 * math.pi / NTH) * radii())
    velocity_out[2] = ustar[2] - turn

    def slab(g, _):
        speed = fluid[g]
        for h in (0, 8):
            rows = second[g, h:h + 8]
            is_rate, rate = rates_of(rows)
            moved = (rows + STEP * rate * speed) / (1.0 + STEP * rate)
            rows = jnp.where(is_rate, rows, moved)
            if flat:
                parcels_out[h:h + 8, pl.ds(pl.multiple_of(g * capacity, 128), capacity)] = rows
            else:
                parcels_out[g, h:h + 8] = rows
        return 0

    lax.fori_loop(0, gz, slab, 0, unroll=gz <= 8)


def body(velocity, viscosity, parcels, dest_rank, dest_cell, counts):
    gz = lax.axis_size("gz")
    pa = lax.axis_size("pa")
    columns = viscosity.shape[2]
    block = parcels.shape[0]
    slots = 3 * block // gz
    capacity = -(-slots // 128) * 128
    flat = capacity == slots
    velocity = velocity.reshape(3, NR, columns)
    viscosity = viscosity.reshape(NR, columns)
    fields = jnp.concatenate([velocity, viscosity[None]], 0)
    above = lax.ppermute(fields, "gz", [(i + 1, i) for i in range(gz - 1)])
    below = lax.ppermute(fields, "gz", [(i, i + 1) for i in range(gz - 1)])
    edges = jnp.concatenate([fields[:, :, 0], fields[:, :, -1]], 0)

    def shape(*s):
        return jax.ShapeDtypeStruct(s, f32)

    plain = pltpu.CompilerParams(vmem_limit_bytes=LIMIT)
    first, second = pl.pallas_call(
        functools.partial(pack_kernel, gz, capacity),
        out_shape=(shape(gz, 8, capacity), shape(gz, 16, capacity)),
        in_specs=[pl.BlockSpec(memory_space=pltpu.SMEM), VM, VM, VM],
        out_specs=(VM, VM),
        compiler_params=plain,
        name="pack",
    )(counts, dest_rank.reshape(1, block), dest_cell.reshape(1, block), parcels.T)
    dma = pltpu.SemaphoreType.DMA
    first, edge_left, edge_right = pl.pallas_call(
        functools.partial(route_kernel, gz, pa),
        out_shape=(shape(gz, 8, capacity), shape(8, NR), shape(8, NR)),
        in_specs=[VM, VM],
        out_specs=(VM, VM, VM),
        scratch_shapes=[dma((gz,)), dma((gz,)), dma((2,)), dma((2,))],
        compiler_params=pltpu.CompilerParams(collective_id=0, has_side_effects=True, vmem_limit_bytes=LIMIT),
        name="route",
    )(first, edges)
    fluid, deposit = pl.pallas_call(
        functools.partial(deposit_kernel, gz),
        out_shape=(shape(gz, 8, capacity), shape(3, NR, columns)),
        in_specs=[VM, VM],
        out_specs=(VM, VM),
        compiler_params=plain,
        name="deposit",
    )(first, velocity)
    where = lax.axis_index("pa").astype(jnp.int32).reshape(1)
    high, low = forward_table(pa)
    chosen = pl.BlockSpec((1, 2 * columns, NTH), lambda i, w: (w[0], 0, 0))
    ustar, partial = pl.pallas_call(
        functools.partial(momentum_kernel, pa),
        out_shape=(shape(3, NR, columns), shape(pa, NR, columns)),
        grid_spec=pltpu.PrefetchScalarGridSpec(
            num_scalar_prefetch=1, grid=(1,),
            in_specs=[VM] * 7 + [chosen, chosen],
            out_specs=(VM, VM)),
        compiler_params=plain,
        name="momentum",
    )(where, velocity, viscosity, above, below, edge_left.T, edge_right.T, deposit, high, low)
    ratios = radial_ratios(pa)
    second, hat = pl.pallas_call(
        functools.partial(solve_kernel, gz, pa),
        out_shape=(shape(gz, 16, capacity), shape(pa, NR, columns)),
        in_specs=[VM, VM, pl.BlockSpec(memory_space=pl.ANY)],
        out_specs=(VM, VM),
        scratch_shapes=[
            pltpu.VMEM((pa - 1, NR, columns), f32), pltpu.VMEM(ratios.shape[1:], f32),
            dma((gz,)), dma((gz,)), dma((pa - 1,)), dma((pa - 1,)), dma((pa - 1,)), dma((pa - 1,)), dma(()),
        ],
        compiler_params=pltpu.CompilerParams(collective_id=1, has_side_effects=True, vmem_limit_bytes=LIMIT),
        name="solve",
    )(second, partial, ratios)
    high, low = inverse_table(pa)
    chosen = pl.BlockSpec((1, 2, NTH, columns), lambda i, w: (w[0], 0, 0, 0))
    velocity_out, parcels_out = pl.pallas_call(
        functools.partial(finish_kernel, gz, pa, flat),
        out_shape=(shape(3, NR, columns), shape(16, gz * slots) if flat else shape(gz, 16, capacity)),
        grid_spec=pltpu.PrefetchScalarGridSpec(
            num_scalar_prefetch=1, grid=(1,),
            in_specs=[VM, VM, chosen, chosen, VM, VM],
            out_specs=(VM, VM)),
        compiler_params=plain,
        name="finish",
    )(where, hat, ustar, high, low, second, fluid)
    if not flat:
        parcels_out = parcels_out[:, :, :slots].transpose(1, 0, 2).reshape(16, gz * slots)
    return velocity_out.reshape(3, 1, NR, columns), parcels_out.T


def solution(mesh):
    in_specs = (
        P(None, "gz", None, "pa"),
        P("gz", None, "pa"),
        P(("gz", "pa"), None),
        P(("gz", "pa"), None),
        P(("gz", "pa")),
        P(("gz", "pa")),
    )
    out_specs = (P(None, "gz", None, "pa"), P(("gz", "pa"), None))
    return jax.shard_map(body, mesh=mesh, in_specs=in_specs, out_specs=out_specs, check_vma=False)
```

time: 132 us -> 53.8 us (0.41); the launches traced: 130 us -> 53.3 us
  Pallas kernels: 0 us -> 36 us
  starting transfers between devices: 31.7 us -> 5.29 us
  matrix products: 25.7 us -> 0 us
  other arithmetic: 24 us -> 2.84 us
  local copies, waits for them, and re-layouts: 27.5 us -> 7.69 us
  waiting for transfers between devices: 10.6 us -> 0.01 us
  blocking collectives: 7.91 us -> 0 us
    pallas_call x0 -> x6, Pallas kernels: none -> 36 us  [the longest x1 18.4 us: body(): pl.pallas_call(functools.partial(solve_kernel, gz, pa), out_shape=(shape(...]
    dot_general x14 -> x0, matrix products: 25.7 us -> none  [the longest x9 7.86 us: deposit_step(): lax.dot_general(left, right, (((0,), (0,)), ((), ())), preferred_element_...]
    all_to_all x5 -> x0, starting transfers between devices: 23.3 us -> none  [the longest x2 8.44 us: to_radial(): return lax.all_to_all(values, 'pa', split_axis=3, concat_axis=2, tiled=True)]
    all_to_all x5 -> x0, waiting for transfers between devices: 10.6 us -> none  [the longest x2 7.04 us: to_radial(): return lax.all_to_all(values, 'pa', split_axis=3, concat_axis=2, tiled=True)]
    scatter x2 -> x0, local copies, waits for them, and re-layouts: 8.91 us -> none  [the longest x1 5.05 us: body(): where_to = jnp.full((slabs * capacity,), -1, jnp.int32).at[place].set(des...]
    all_to_all x1 -> x0, blocking collectives: 7.91 us -> none  [to_theta(): return lax.all_to_all(values, 'pa', split_axis=2, concat_axis=3, tiled=True)]
    slice x46 -> x0, local copies, waits for them, and re-layouts: 4.65 us -> none  [the longest x2 3.16 us: padded_2(): first = lax.slice_in_dim(x, 0, width, axis=dim)]
    unnamed x4 -> x0, other arithmetic: 3.8 us -> none
  transfers between devices with their start and end apart: 9 -> 2, of which waited for: 3 -> 0; matrix products, arithmetic and copies ran while one was open for 31% -> 4% of each run, Pallas kernels for 0% -> 29%
where the time goes in v1:
time: 53.8 us; the launch traced here: 53.3 us
  Pallas kernels  36 us (67%)
  local copies, waits for them, and re-layouts  7.69 us (14%)
  starting transfers between devices  5.29 us (10%)
  other arithmetic  2.84 us (5%)
  between operations  1.43 us (3%)
    pallas_call x1, Pallas kernels, body(): pl.pallas_call(functools.partial(solve_kernel, gz, pa), out_shape=(shape(...  18.4 us
    pallas_call x1, Pallas kernels, body(): pl.pallas_call(functools.partial(route_kernel, gz, pa), out_shape=(shape(...  10.1 us
    unnamed x20, local copies, waits for them, and re-layouts  7.48 us
    ppermute x1, starting transfers between devices, body(): below = lax.ppermute(fields, 'gz', [(i, i + 1) for i in range(gz - 1)])  4 us
    pallas_call x1, Pallas kernels, body(): pl.pallas_call(functools.partial(deposit_kernel, gz), out_shape=(shape(gz...  3.82 us
    slice x1, other arithmetic, body(): edges = jnp.concatenate([fields[:, :, 0], fields[:, :, -1]], 0)  1.71 us
    pallas_call x1, Pallas kernels, body(): pl.pallas_call(functools.partial(pack_kernel, gz, capacity), out_shape=(s...  1.41 us
    pallas_call x1, Pallas kernels, body(): pl.pallas_call(functools.partial(finish_kernel, gz, pa, flat), out_shape=...  1.3 us
  transfers between devices with their start and end apart: 2, of which 0 were waited for; matrix products, arithmetic and copies ran while one was open for 4% of the time, Pallas kernels for 29%

profile of v1, /device:TPU:1, one launch (start us, length us, event | category | flops | bytes accessed | tf_op | source)
XLA Modules:
  0.0 53.3 jit_solution(17264520699168908699)
XLA Ops:
  0.6 0.0 copy-start.2
  0.6 1.1 %pad_maximum_fusion = f32[4,192,128]{2,1,0:T(8,128)S(1)} fusion(f32[1,192,128]{2,1,0:T(8,128)} %param.12, f32[3,192,128]{2,1,0:T(8,128)} %bitcast.12), kind=kLoop, calls=%fused_computation.2 | loop fusion | flops 98304 | bytes 786432 | tf_op jit(solution)/shard_map/concatenate | solution.py:393
  1.8 4.0 %collective-permute-start.1 = (f32[4,192,128]{2,1,0:T(8,128)S(1)}, f32[4,192,128]{2,1,0:T(8,128)S(1)}, u32[]{:S(2)}, u32[]{:S(2)}) collective-permute-start(f32[4,192,128]{2,1,0:T(8,128)S(1)} %pad_maximum_fusion), channel_id=1, source_target_pairs={{0,4},{4,8},{8,12},{12,16},{16,20},{20,24},{24,28},{1,5},{5,9},{9,... | collective-permute-start | bytes 1179656 | tf_op jit(solution)/shard_map/ppermute | solution.py:395
  5.8 1.3 %collective-permute-start = (f32[4,192,128]{2,1,0:T(8,128)S(1)}, f32[4,192,128]{2,1,0:T(8,128)S(1)}, u32[]{:S(2)}, u32[]{:S(2)}) collective-permute-start(f32[4,192,128]{2,1,0:T(8,128)S(1)} %pad_maximum_fusion), channel_id=1, source_target_pairs={{4,0},{8,4},{12,8},{16,12},{20,16},{24,20},{28,24},{5,1},{9,5},{13... | collective-permute-start | bytes 1179656 | tf_op jit(solution)/shard_map/ppermute | solution.py:394
  7.7 0.0 copy-start.7
  7.7 0.8 %copy-done.7 = f32[1024,16]{0,1:T(8,128)S(1)} copy-done((f32[1024,16]{0,1:T(8,128)S(1)}, f32[1024,16]{0,1:T(8,128)}, u32[]{:S(2)}) %copy-start.7) | copy-done | bytes 65560
  8.6 0.7 %copy-done.8 = s32[1024,1]{0,1:T(1,128)S(1)} copy-done((s32[1024,1]{0,1:T(1,128)S(1)}, s32[1024,1]{0,1:T(1,128)}, u32[]{:S(2)}) %copy-start.8) | copy-done | bytes 4120
  9.3 0.7 %copy-done.9 = s32[1024]{0:T(1024)S(1)} copy-done((s32[1024]{0:T(1024)S(1)}, s32[1024]{0:T(1024)}, u32[]{:S(2)}) %copy-start.9) | copy-done | bytes 4120
  9.9 1.4 %pack.1 = (f32[8,8,384]{2,1,0:T(8,128)S(1)}, f32[8,16,384]{2,1,0:T(8,128)S(1)}) custom-call(s32[1]{0:T(128)S(6)} %copy.23.counts, s32[1,1024]{1,0:T(1,128)S(1)} %bitcast.20, s32[1,1024]{1,0:T(1,128)S(1)} %bitcast.21, f32[16,1024]{1,0:T(8,128)S(1)} %bitcast.19), custom_call_target="tpu_custom_call" | custom-call | tf_op jit(solution)/shard_map/pack/pallas_call | solution.py:402
  11.4 1.7 %fusion.1 = (f32[4,192]{1,0:T(4,128)S(1)}, f32[4,192]{1,0:T(4,128)S(1)}) fusion(f32[3,192,128]{2,1,0:T(8,128)} %bitcast.13, f32[1,192,128]{2,1,0:T(8,128)} %param.12), kind=kLoop, calls=%fused_computation.6 | loop fusion | flops 1536 | bytes 399360 | tf_op jit(solution)/shard_map/slice | solution.py:396
  13.1 10.1 %route.1 = (f32[8,8,384]{2,1,0:T(8,128)S(1)}, f32[8,192]{1,0:T(8,128)S(1)}, f32[8,192]{1,0:T(8,128)S(1)}) custom-call(f32[8,8,384]{2,1,0:T(8,128)S(1)} %get-tuple-element.16.first, f32[8,192]{1,0:T(8,128)S(1)} %pad_maximum_fusion.1.edges), custom_call_target="tpu_custom_call" | custom-call | tf_op jit(solution)/shard_map/route/pallas_call | solution.py:411
  23.2 0.1 copy.20
  23.3 0.1 copy.21
  23.4 0.0 copy-start
  23.5 1.0 %copy-done = f32[3,1,192,128]{3,2,1,0:T(8,128)S(1)} copy-done((f32[3,1,192,128]{3,2,1,0:T(8,128)S(1)}, f32[3,1,192,128]{3,2,1,0:T(8,128)}, u32[]{:S(2)}) %copy-start) | copy-done | bytes 294936
  24.4 3.8 %deposit.1 = (f32[8,8,384]{2,1,0:T(8,128)S(1)}, f32[3,192,128]{2,1,0:T(8,128)S(1)}) custom-call(f32[8,8,384]{2,1,0:T(8,128)S(1)} %get-tuple-element.19.first, f32[3,192,128]{2,1,0:T(8,128)S(1)} %bitcast.14), custom_call_target="tpu_custom_call" | custom-call | tf_op jit(solution)/shard_map/deposit/pallas_call | solution.py:420
  28.3 0.0 copy-start.1
  28.3 1.0 %copy-done.1 = f32[3,1,192,128]{3,2,1,0:T(8,128)S(1)} copy-done((f32[3,1,192,128]{3,2,1,0:T(8,128)S(1)}, f32[3,1,192,128]{3,2,1,0:T(8,128)}, u32[]{:S(2)}) %copy-start.1) | copy-done | bytes 294936
  29.2 1.2 %copy-done.4 = bf16[4,256,512]{2,1,0:T(8,128)(2,1)S(1)} copy-done((bf16[4,256,512]{2,1,0:T(8,128)(2,1)S(1)}, bf16[4,256,512]{2,1,0:T(8,128)(2,1)}, u32[]{:S(2)}) %copy-start.4) | copy-done | bytes 1048600
  30.5 1.2 %copy-done.5 = bf16[4,256,512]{2,1,0:T(8,128)(2,1)S(1)} copy-done((bf16[4,256,512]{2,1,0:T(8,128)(2,1)S(1)}, bf16[4,256,512]{2,1,0:T(8,128)(2,1)}, u32[]{:S(2)}) %copy-start.5) | copy-done | bytes 1048600
  31.7 0.9 %copy-done.6 = f32[1,192,128]{2,1,0:T(8,128)S(1)} copy-done((f32[1,192,128]{2,1,0:T(8,128)S(1)}, f32[1,192,128]{2,1,0:T(8,128)}, u32[]{:S(2)}) %copy-start.6) | copy-done | bytes 98328
  32.6 1.0 %momentum.1 = (f32[3,192,128]{2,1,0:T(8,128)S(1)}, f32[4,192,128]{2,1,0:T(8,128)S(1)}) custom-call(s32[1]{0:T(128)} %bitcast.where, f32[3,192,128]{2,1,0:T(8,128)S(1)} %bitcast.15, f32[192,128]{1,0:T(8,128)S(1)} %bitcast.16, f32[4,192,128]{2,1,0:T(8,128)S(1)} %collective-permute-done.above, f32[4,192,128]{2,1,0:T(8,128)S(1)} %collective-permute-done.1.below, ...), custom_call_target="tpu_custom_call" | custom-call | tf_op jit(solution)/shard_map/momentum/pallas_call | solution.py:431
  33.5 18.4 %solve.1 = (f32[8,16,384]{2,1,0:T(8,128)S(1)}, f32[4,192,128]{2,1,0:T(8,128)S(1)}) custom-call(f32[8,16,384]{2,1,0:T(8,128)S(1)} %get-tuple-element.15.second, f32[4,192,128]{2,1,0:T(8,128)S(1)} %get-tuple-element.21.partial, f32[4,17,192,128]{3,2,1,0:T(8,128)} %constant.16.clone.ratios), custom_call_target="tpu_custom_call" | custom-call | tf_op jit(solution)/shard_map/solve/pallas_call | solution.py:442
  52.0 1.3 %finish.1 = (f32[3,192,128]{2,1,0:T(8,128)}, f32[16,3072]{1,0:T(8,128)}) custom-call(s32[1]{0:T(128)} %bitcast.where, f32[4,192,128]{2,1,0:T(8,128)S(1)} %get-tuple-element.22.hat, f32[3,192,128]{2,1,0:T(8,128)S(1)} %get-tuple-element.23.ustar, bf16[4,2,512,128]{3,2,1,0:T(8,128)(2,1)S(1)} %copy-done.3, bf16[4,2,512,128]{3,2,1,0:T(8,128)(2,1)S(1)} %copy-done.2, ...), custom_call_target="tpu_custom_call" | custom-call | tf_op jit(solution)/shard_map/finish/pallas_call | solution.py:456
  (11 shorter events, 0.0 us)
Async XLA Ops:
  0.6 51.3 %copy-start.2 = (bf16[4,2,512,128]{3,2,1,0:T(8,128)(2,1)S(1)}, bf16[4,2,512,128]{3,2,1,0:T(8,128)(2,1)}, u32[]{:S(2)}) copy-start(bf16[4,2,512,128]{3,2,1,0:T(8,128)(2,1)} %constant.18.clone.low) | copy-start | bytes 3145732
  1.8 26.5 %collective-permute-start.1 = (f32[4,192,128]{2,1,0:T(8,128)S(1)}, f32[4,192,128]{2,1,0:T(8,128)S(1)}, u32[]{:S(2)}, u32[]{:S(2)}) collective-permute-start(f32[4,192,128]{2,1,0:T(8,128)S(1)} %pad_maximum_fusion), channel_id=1, source_target_pairs={{0,4},{4,8},{8,12},{12,16},{16,20},{20,24},{24,28},{1,5},{5,9},{9,... | collective-permute-start | bytes 1179656 | tf_op jit(solution)/shard_map/ppermute | solution.py:395
  5.8 22.5 %collective-permute-start = (f32[4,192,128]{2,1,0:T(8,128)S(1)}, f32[4,192,128]{2,1,0:T(8,128)S(1)}, u32[]{:S(2)}, u32[]{:S(2)}) collective-permute-start(f32[4,192,128]{2,1,0:T(8,128)S(1)} %pad_maximum_fusion), channel_id=1, source_target_pairs={{4,0},{8,4},{12,8},{16,12},{20,16},{24,20},{28,24},{5,1},{9,5},{13... | collective-permute-start | bytes 1179656 | tf_op jit(solution)/shard_map/ppermute | solution.py:394
  7.7 0.8 %copy-start.7 = (f32[1024,16]{0,1:T(8,128)S(1)}, f32[1024,16]{0,1:T(8,128)}, u32[]{:S(2)}) copy-start(f32[1024,16]{0,1:T(8,128)} %param.13) | copy-start | bytes 196612
  8.6 0.7 %copy-start.8 = (s32[1024,1]{0,1:T(1,128)S(1)}, s32[1024,1]{0,1:T(1,128)}, u32[]{:S(2)}) copy-start(s32[1024,1]{0,1:T(1,128)} %param.14) | copy-start | bytes 12292
  9.3 0.7 %copy-start.9 = (s32[1024]{0:T(1024)S(1)}, s32[1024]{0:T(1024)}, u32[]{:S(2)}) copy-start(s32[1024]{0:T(1024)} %param.15) | copy-start | bytes 12292
  23.4 1.0 %copy-start = (f32[3,1,192,128]{3,2,1,0:T(8,128)S(1)}, f32[3,1,192,128]{3,2,1,0:T(8,128)}, u32[]{:S(2)}) copy-start(f32[3,1,192,128]{3,2,1,0:T(8,128)} %param.11) | copy-start | bytes 884740
  28.3 1.0 %copy-start.1 = (f32[3,1,192,128]{3,2,1,0:T(8,128)S(1)}, f32[3,1,192,128]{3,2,1,0:T(8,128)}, u32[]{:S(2)}) copy-start(f32[3,1,192,128]{3,2,1,0:T(8,128)} %param.11) | copy-start | bytes 884740
  29.2 1.2 %copy-start.4 = (bf16[4,256,512]{2,1,0:T(8,128)(2,1)S(1)}, bf16[4,256,512]{2,1,0:T(8,128)(2,1)}, u32[]{:S(2)}) copy-start(bf16[4,256,512]{2,1,0:T(8,128)(2,1)} %constant.15.clone.low) | copy-start | bytes 3145732
  30.5 1.2 %copy-start.5 = (bf16[4,256,512]{2,1,0:T(8,128)(2,1)S(1)}, bf16[4,256,512]{2,1,0:T(8,128)(2,1)}, u32[]{:S(2)}) copy-start(bf16[4,256,512]{2,1,0:T(8,128)(2,1)} %constant.14.clone.high) | copy-start | bytes 3145732
  31.7 0.9 %copy-start.6 = (f32[1,192,128]{2,1,0:T(8,128)S(1)}, f32[1,192,128]{2,1,0:T(8,128)}, u32[]{:S(2)}) copy-start(f32[1,192,128]{2,1,0:T(8,128)} %param.12) | copy-start | bytes 294916
  32.6 19.4 %copy-start.3 = (bf16[4,2,512,128]{3,2,1,0:T(8,128)(2,1)S(1)}, bf16[4,2,512,128]{3,2,1,0:T(8,128)(2,1)}, u32[]{:S(2)}) copy-start(bf16[4,2,512,128]{3,2,1,0:T(8,128)(2,1)} %constant.17.clone.high) | copy-start | bytes 3145732

commit v2 on v1

--- a/solution.py
+++ b/solution.py
@@ -14,7 +14,7 @@
 NTH = 512
 STEP = 0.1
 SHIFT = 0.0001
-LIMIT = 48 * 1024 * 1024
+LIMIT = 56 * 1024 * 1024
 MESH = pl.DeviceIdType.MESH
 f32 = jnp.float32
 bf16 = jnp.bfloat16
@@ -109,8 +109,17 @@
     return is_rate, w + rolled(w, 1) + rolled(w, 2) + rolled(w, 3)
 
 
-def pack_kernel(gz, capacity, counts, rank, cell, parcels, first, second):
+def loop(first, last, step):
+    if last - first <= 8:
+        for i in range(first, last):
+            step(i)
+    else:
+        lax.fori_loop(first, last, lambda i, _: (step(i), 0)[1], 0)
+
+
+def pack(gz, counts, rank, cell, parcels, first, second):
     block = rank.shape[1]
+    capacity = first.shape[2]
     tiles = capacity // 128
     live = iota((1, block), 1) < counts[0]
     target = jnp.where(live, rank[...], gz)
@@ -137,7 +146,7 @@
     column = (cells & 127).astype(f32)
     table = jnp.concatenate([one, two, three, line, column, jnp.zeros((14, block), f32)], 0)
 
-    def slab(g, _):
+    def slab(g):
         left = [jnp.where(high == g * tiles + i, table, 0.0).astype(bf16) for i in range(tiles)]
         got = lax.dot_general(jnp.concatenate(left, 0), low_hot, (((1,), (1,)), ((), ())), preferred_element_type=f32)
         for i in range(tiles):
@@ -153,89 +162,32 @@
                 total = total + jnp.where(is_rate, weight, weight * half)
             total = total + rolled(total, 4)
             first[g, :, lanes] = jnp.where(iota(total.shape, 0) == 4, code, total)
-        return 0
-
-    lax.fori_loop(0, gz, slab, 0, unroll=gz <= 8)
-
-
-def loop(first, last, step):
-    if last - first <= 8:
-        for i in range(first, last):
-            step(i)
-    else:
-        lax.fori_loop(first, last, lambda i, _: (step(i), 0)[1], 0)
-
-
-def route_kernel(gz, pa, first, edges, first_out, left_out, right_out, send, recv, esend, erecv):
-    me = lax.axis_index("gz")
-    mp = lax.axis_index("pa")
-    right = lax.rem(mp + 1, pa)
-    left = lax.rem(mp + pa - 1, pa)
-    barrier = pltpu.get_barrier_semaphore()
-
-    def greet(o):
-        pl.semaphore_signal(barrier, inc=1, device_id=(lax.rem(me + o, gz), mp), device_id_type=MESH)
-
-    loop(1, gz, greet)
-    for q in (left, right):
-        pl.semaphore_signal(barrier, inc=1, device_id=(me, q), device_id_type=MESH)
-    pl.semaphore_wait(barrier, gz + 1)
-
-    def copy(o):
-        to = lax.rem(me + o, gz)
-        return pltpu.make_async_remote_copy(
-            src_ref=first.at[to], dst_ref=first_out.at[me], send_sem=send.at[o], recv_sem=recv.at[o],
-            device_id=(to, mp), device_id_type=MESH)
-
-    to_right = pltpu.make_async_remote_copy(
-        src_ref=edges, dst_ref=left_out, send_sem=esend.at[0], recv_sem=erecv.at[0],
-        device_id=(me, right), device_id_type=MESH)
-    to_left = pltpu.make_async_remote_copy(
-        src_ref=edges, dst_ref=right_out, send_sem=esend.at[1], recv_sem=erecv.at[1],
-        device_id=(me, left), device_id_type=MESH)
-    loop(1, gz, lambda o: copy(o).start())
-    to_right.start()
-    to_left.start()
-    first_out[me] = first[me]
-    loop(1, gz, lambda o: copy(o).wait())
-    to_right.wait()
-    to_left.wait()
-
-
-def deposit_kernel(gz, first, velocity, fluid, deposit):
-    columns = velocity.shape[2]
-    capacity = first.shape[2]
-    pieces = []
+
+    loop(0, gz, slab)
+
+
+def deposit_slab(g, came, turned, fluid, deposit):
+    columns = deposit.shape[2]
+    rows = came[g]
+    capacity = rows.shape[1]
+    code = rows[4:5].astype(jnp.int32)
+    line = (code >> 7) - 1
+    column = code & 127
+    line_hot = (iota((NR, capacity), 0) == line).astype(f32).astype(bf16)
+    column_hot = iota((columns, capacity), 0) == column
+    picked = jnp.dot(turned, line_hot, preferred_element_type=f32)
+    looked, pushes = [], []
     for c in range(3):
-        turned = velocity[c].T
-        top = turned.astype(bf16)
-        pieces += [top, (turned - top.astype(f32)).astype(bf16)]
-    turned = jnp.concatenate(pieces, 0)
-    deposit[...] = jnp.zeros_like(deposit)
-
-    def slab(g, _):
-        rows = first[g]
-        code = rows[4:5].astype(jnp.int32)
-        line = (code >> 7) - 1
-        column = code & 127
-        line_hot = (iota((NR, capacity), 0) == line).astype(f32).astype(bf16)
-        column_hot = iota((columns, capacity), 0) == column
-        picked = jnp.dot(turned, line_hot, preferred_element_type=f32)
-        looked, pushes = [], []
-        for c in range(3):
-            both = picked[2 * c * columns:(2 * c + 1) * columns] + picked[(2 * c + 1) * columns:(2 * c + 2) * columns]
-            speed = jnp.sum(jnp.where(column_hot, both, 0.0), axis=0, keepdims=True)
-            drag = (rows[c:c + 1] - speed * rows[3:4]).astype(bf16).astype(f32)
-            looked.append(speed)
-            pushes.append(jnp.where(column_hot, drag, 0.0).astype(bf16))
-        nothing = jnp.zeros_like(looked[0])
-        fluid[g] = jnp.concatenate((looked + [nothing]) * 2, 0)
-        added = lax.dot_general(line_hot, jnp.concatenate(pushes, 0), (((1,), (1,)), ((), ())), preferred_element_type=f32)
-        for c in range(3):
-            deposit[c] += added[:, c * columns:(c + 1) * columns]
-        return 0
-
-    lax.fori_loop(0, gz, slab, 0, unroll=gz <= 8)
+        both = picked[2 * c * columns:(2 * c + 1) * columns] + picked[(2 * c + 1) * columns:(2 * c + 2) * columns]
+        speed = jnp.sum(jnp.where(column_hot, both, 0.0), axis=0, keepdims=True)
+        drag = (rows[c:c + 1] - speed * rows[3:4]).astype(bf16).astype(f32)
+        looked.append(speed)
+        pushes.append(jnp.where(column_hot, drag, 0.0).astype(bf16))
+    nothing = jnp.zeros_like(looked[0])
+    fluid[g] = jnp.concatenate((looked + [nothing]) * 2, 0)
+    added = lax.dot_general(line_hot, jnp.concatenate(pushes, 0), (((1,), (1,)), ((), ())), preferred_element_type=f32)
+    for c in range(3):
+        deposit[c] += added[:, c * columns:(c + 1) * columns]
 
 
 def split_dot(x, high, low):
@@ -245,8 +197,8 @@
     return out + jnp.dot(top, high, preferred_element_type=f32)
 
 
-def momentum_kernel(pa, where, velocity, viscosity, above, below, edge_left, edge_right, deposit, high, low, ustar, partial):
-    columns = velocity.shape[2]
+def momentum(pa, speeds, viscosity, above, below, edge_left, edge_right, deposit, high, low, ustar, partial):
+    columns = speeds.shape[2]
     radius = radii()
     arc = 1.0 / (radius * (2.0 * math.pi / NTH)) ** 2
     nu = viscosity[...]
@@ -275,7 +227,7 @@
     ]
     new = []
     for c in range(3):
-        u = velocity[c]
+        u = speeds[c]
         sides = (above[c], below[c], outward(u), inward(u), ahead(u, c), behind(u, c))
         total = weights[0] * (sides[0] - u)
         for w, s in zip(weights[1:], sides[1:]):
@@ -286,17 +238,27 @@
     flux = jnp.where(row == NR - 1, 0.0, (radius + 0.5) * 0.5 * (radial + outward(radial)))
     divergence = (flux - inward(flux)) / radius
     across = new[2] / (2.0 * (2.0 * math.pi / NTH) * radius)
-    out = split_dot(jnp.concatenate([divergence, across], 1), high[0], low[0])
+    out = split_dot(jnp.concatenate([divergence, across], 1), high[...], low[...])
     for q in range(pa):
         partial[q] = out[:, q * columns:(q + 1) * columns]
 
 
-def solve_kernel(gz, pa, second, partial, ratios, second_out, hat, came, held, send, recv, rsend, rrecv, gsend, grecv, lsem):
+def main_kernel(gz, pa, counts, rank_in, cell_in, parcels_in, velocity, viscosity, high_in, low_in, ratios,
+                ustar, hat, second_in, fluid,
+                rank, cell, parcels, speeds, nu, high, low, held, first, second, first_in,
+                above, below, edges, edge_left, edge_right, deposit, partial, came,
+                lsem, fsend, frecv, send, recv, zsend, zrecv, esend, erecv, rsend, rrecv, gsend, grecv):
     me = lax.axis_index("gz")
     mp = lax.axis_index("pa")
-    columns = partial.shape[2]
-    load = pltpu.make_async_copy(ratios.at[mp], held, lsem)
-    load.start()
+    columns = nu.shape[1]
+    loads = [
+        pltpu.make_async_copy(a, b, lsem.at[i])
+        for i, (a, b) in enumerate((
+            (rank_in, rank), (cell_in, cell), (parcels_in, parcels), (velocity, speeds), (viscosity.at[0], nu),
+            (high_in.at[mp], high), (low_in.at[mp], low), (ratios.at[mp], held)))
+    ]
+    for c in loads:
+        c.start()
     barrier = pltpu.get_barrier_semaphore()
 
     def greet(o):
@@ -306,8 +268,101 @@
     others = [lax.rem(mp + o, pa) for o in range(1, pa)]
     for q in others:
         pl.semaphore_signal(barrier, inc=1, device_id=(me, q), device_id_type=MESH)
+    for c in loads[:5]:
+        c.wait()
+    pack(gz, counts, rank, cell, parcels, first, second)
     pl.semaphore_wait(barrier, gz + pa - 2)
 
+    def slab_copy(source, target, ssem, rsem, o):
+        to = lax.rem(me + o, gz)
+        return pltpu.make_async_remote_copy(
+            src_ref=source.at[to], dst_ref=target.at[me], send_sem=ssem.at[o], recv_sem=rsem.at[o],
+            device_id=(to, mp), device_id_type=MESH)
+
+    def first_copy(o):
+        return slab_copy(first, first_in, fsend, frecv, o)
+
+    def second_copy(o):
+        return slab_copy(second, second_in, send, recv, o)
+
+    loop(1, gz, lambda o: first_copy(o).start())
+
+    def plane(source, target, part, i, to):
+        return pltpu.make_async_remote_copy(
+            src_ref=source, dst_ref=target.at[part], send_sem=zsend.at[i], recv_sem=zrecv.at[i],
+            device_id=(to, mp), device_id_type=MESH)
+
+    up, down = lax.rem(me + 1, gz), lax.rem(me + gz - 1, gz)
+    to_up = [plane(velocity, below, pl.ds(0, 3), 0, up), plane(viscosity, below, pl.ds(3, 1), 1, up)]
+    to_down = [plane(velocity, above, pl.ds(0, 3), 2, down), plane(viscosity, above, pl.ds(3, 1), 3, down)]
+
+    @pl.when(me < gz - 1)
+    def _():
+        for c in to_up:
+            c.start()
+
+    @pl.when(me > 0)
+    def _():
+        for c in to_down:
+            c.start()
+
+    pieces, ends = [], []
+    for c in range(3):
+        turned = speeds[c].T
+        top = turned.astype(bf16)
+        pieces += [top, (turned - top.astype(f32)).astype(bf16)]
+        ends.append(turned)
+    ends.append(nu[...].T)
+    edges[...] = jnp.concatenate([x[:1] for x in ends] + [x[columns - 1:] for x in ends], 0)
+    right, left = lax.rem(mp + 1, pa), lax.rem(mp + pa - 1, pa)
+    sides = [
+        pltpu.make_async_remote_copy(
+            src_ref=edges, dst_ref=target, send_sem=esend.at[i], recv_sem=erecv.at[i],
+            device_id=(me, q), device_id_type=MESH)
+        for i, (target, q) in enumerate(((edge_left, right), (edge_right, left)))
+    ]
+    for c in sides:
+        c.start()
+    loop(1, gz, lambda o: second_copy(o).start())
+    turned = jnp.concatenate(pieces, 0)
+    deposit[...] = jnp.zeros_like(deposit)
+    first_in[me] = first[me]
+    second_in[me] = second[me]
+    deposit_slab(me, first_in, turned, fluid, deposit)
+
+    def take(o):
+        first_copy(o).wait()
+        deposit_slab(lax.rem(me + gz - o, gz), first_in, turned, fluid, deposit)
+
+    loop(1, gz, take)
+    for c in sides:
+        c.wait()
+    for c in loads[5:]:
+        c.wait()
+
+    @pl.when(me < gz - 1)
+    def _():
+        for c in to_up:
+            c.wait_send()
+        for c in to_down:
+            c.wait_recv()
+
+    @pl.when(me == gz - 1)
+    def _():
+        above[...] = jnp.zeros_like(above)
+
+    @pl.when(me > 0)
+    def _():
+        for c in to_down:
+            c.wait_send()
+        for c in to_up:
+            c.wait_recv()
+
+    @pl.when(me == 0)
+    def _():
+        below[...] = jnp.zeros_like(below)
+
+    momentum(pa, speeds, nu, above, below, edge_left[...].T, edge_right[...].T, deposit, high, low, ustar, partial)
     sums = [
         pltpu.make_async_remote_copy(
             src_ref=partial.at[q], dst_ref=came.at[i], send_sem=rsend.at[i], recv_sem=rrecv.at[i],
@@ -316,16 +371,6 @@
     ]
     for c in sums:
         c.start()
-
-    def copy(o):
-        to = lax.rem(me + o, gz)
-        return pltpu.make_async_remote_copy(
-            src_ref=second.at[to], dst_ref=second_out.at[me], send_sem=send.at[o], recv_sem=recv.at[o],
-            device_id=(to, mp), device_id_type=MESH)
-
-    loop(1, gz, lambda o: copy(o).start())
-    second_out[me] = second[me]
-    load.wait()
     for c in sums:
         c.wait()
     x = partial[mp]
@@ -352,7 +397,7 @@
         c.start()
     for c in spread:
         c.wait()
-    loop(1, gz, lambda o: copy(o).wait())
+    loop(1, gz, lambda o: second_copy(o).wait())
 
 
 def finish_kernel(gz, pa, flat, where, hat, ustar, high, low, second, fluid, velocity_out, parcels_out):
@@ -389,68 +434,39 @@
     capacity = -(-slots // 128) * 128
     flat = capacity == slots
     velocity = velocity.reshape(3, NR, columns)
-    viscosity = viscosity.reshape(NR, columns)
-    fields = jnp.concatenate([velocity, viscosity[None]], 0)
-    above = lax.ppermute(fields, "gz", [(i + 1, i) for i in range(gz - 1)])
-    below = lax.ppermute(fields, "gz", [(i, i + 1) for i in range(gz - 1)])
-    edges = jnp.concatenate([fields[:, :, 0], fields[:, :, -1]], 0)
 
     def shape(*s):
         return jax.ShapeDtypeStruct(s, f32)
 
     plain = pltpu.CompilerParams(vmem_limit_bytes=LIMIT)
-    first, second = pl.pallas_call(
-        functools.partial(pack_kernel, gz, capacity),
-        out_shape=(shape(gz, 8, capacity), shape(gz, 16, capacity)),
-        in_specs=[pl.BlockSpec(memory_space=pltpu.SMEM), VM, VM, VM],
-        out_specs=(VM, VM),
-        compiler_params=plain,
-        name="pack",
-    )(counts, dest_rank.reshape(1, block), dest_cell.reshape(1, block), parcels.T)
     dma = pltpu.SemaphoreType.DMA
-    first, edge_left, edge_right = pl.pallas_call(
-        functools.partial(route_kernel, gz, pa),
-        out_shape=(shape(gz, 8, capacity), shape(8, NR), shape(8, NR)),
-        in_specs=[VM, VM],
-        out_specs=(VM, VM, VM),
-        scratch_shapes=[dma((gz,)), dma((gz,)), dma((2,)), dma((2,))],
-        compiler_params=pltpu.CompilerParams(collective_id=0, has_side_effects=True, vmem_limit_bytes=LIMIT),
-        name="route",
-    )(first, edges)
-    fluid, deposit = pl.pallas_call(
-        functools.partial(deposit_kernel, gz),
-        out_shape=(shape(gz, 8, capacity), shape(3, NR, columns)),
-        in_specs=[VM, VM],
-        out_specs=(VM, VM),
-        compiler_params=plain,
-        name="deposit",
-    )(first, velocity)
     where = lax.axis_index("pa").astype(jnp.int32).reshape(1)
     high, low = forward_table(pa)
-    chosen = pl.BlockSpec((1, 2 * columns, NTH), lambda i, w: (w[0], 0, 0))
-    ustar, partial = pl.pallas_call(
-        functools.partial(momentum_kernel, pa),
-        out_shape=(shape(3, NR, columns), shape(pa, NR, columns)),
-        grid_spec=pltpu.PrefetchScalarGridSpec(
-            num_scalar_prefetch=1, grid=(1,),
-            in_specs=[VM] * 7 + [chosen, chosen],
-            out_specs=(VM, VM)),
-        compiler_params=plain,
-        name="momentum",
-    )(where, velocity, viscosity, above, below, edge_left.T, edge_right.T, deposit, high, low)
     ratios = radial_ratios(pa)
-    second, hat = pl.pallas_call(
-        functools.partial(solve_kernel, gz, pa),
-        out_shape=(shape(gz, 16, capacity), shape(pa, NR, columns)),
-        in_specs=[VM, VM, pl.BlockSpec(memory_space=pl.ANY)],
-        out_specs=(VM, VM),
+    ANY = pl.BlockSpec(memory_space=pl.ANY)
+
+    def hold(*s):
+        return pltpu.VMEM(s, f32)
+
+    ustar, hat, second, fluid = pl.pallas_call(
+        functools.partial(main_kernel, gz, pa),
+        out_shape=(shape(3, NR, columns), shape(pa, NR, columns), shape(gz, 16, capacity), shape(gz, 8, capacity)),
+        in_specs=[pl.BlockSpec(memory_space=pltpu.SMEM)] + [ANY] * 8,
+        out_specs=(VM,) * 4,
         scratch_shapes=[
-            pltpu.VMEM((pa - 1, NR, columns), f32), pltpu.VMEM(ratios.shape[1:], f32),
-            dma((gz,)), dma((gz,)), dma((pa - 1,)), dma((pa - 1,)), dma((pa - 1,)), dma((pa - 1,)), dma(()),
+            pltpu.VMEM((1, block), jnp.int32), pltpu.VMEM((1, block), jnp.int32), hold(16, block),
+            hold(3, NR, columns), hold(NR, columns),
+            pltpu.VMEM((2 * columns, NTH), bf16), pltpu.VMEM((2 * columns, NTH), bf16), hold(*ratios.shape[1:]),
+            hold(gz, 8, capacity), hold(gz, 16, capacity), hold(gz, 8, capacity),
+            hold(4, NR, columns), hold(4, NR, columns), hold(8, NR), hold(8, NR), hold(8, NR),
+            hold(3, NR, columns), hold(pa, NR, columns), hold(pa - 1, NR, columns),
+            dma((8,)), dma((gz,)), dma((gz,)), dma((gz,)), dma((gz,)), dma((4,)), dma((4,)), dma((2,)), dma((2,)),
+            dma((pa - 1,)), dma((pa - 1,)), dma((pa - 1,)), dma((pa - 1,)),
         ],
-        compiler_params=pltpu.CompilerParams(collective_id=1, has_side_effects=True, vmem_limit_bytes=LIMIT),
-        name="solve",
-    )(second, partial, ratios)
+        compiler_params=pltpu.CompilerParams(collective_id=0, has_side_effects=True, vmem_limit_bytes=LIMIT),
+        name="step",
+    )(counts, dest_rank.reshape(1, block), dest_cell.reshape(1, block), parcels.T, velocity,
+      viscosity, high, low, ratios)
     high, low = inverse_table(pa)
     chosen = pl.BlockSpec((1, 2, NTH, columns), lambda i, w: (w[0], 0, 0, 0))
     velocity_out, parcels_out = pl.pallas_call(

time: 53.8 us -> 43.5 us (0.81)
  local copies, waits for them, and re-layouts: 7.69 us -> 0 us
  Pallas kernels: 36 us -> 42.1 us
  starting transfers between devices: 5.29 us -> 0 us
  other arithmetic: 2.84 us -> 0 us
    unnamed x20 -> x0, local copies, waits for them, and re-layouts: 7.48 us -> none
    ppermute x2 -> x0, starting transfers between devices: 5.29 us -> none  [the longest x1 4 us: body(): below = lax.ppermute(fields, 'gz', [(i, i + 1) for i in range(gz - 1)])]
    pallas_call x5 -> x1, Pallas kernels: 34.7 us -> 39.5 us  [body(): pl.pallas_call(functools.partial(main_kernel, gz, pa), out_shape=(shape(3...]
    slice x1 -> x0, other arithmetic: 1.71 us -> none  [body(): edges = jnp.concatenate([fields[:, :, 0], fields[:, :, -1]], 0)]
    pallas_call x1, Pallas kernels: 1.3 us -> 2.62 us  [body(): pl.pallas_call(functools.partial(finish_kernel, gz, pa, flat), out_shape=...]
    concatenate x2 -> x0, other arithmetic: 1.13 us -> none  [the longest x1 1.13 us: body(): fields = jnp.concatenate([velocity, viscosity[None]], 0)]
  transfers between devices with their start and end apart: 2 -> 0, of which waited for: 0 -> 0; matrix products, arithmetic and copies ran while one was open for 4% -> 0% of each run, Pallas kernels for 29% -> 0%
where the time goes in v2:
time: 43.5 us; the launch traced here: 43.4 us
  Pallas kernels  42.1 us (97%)
  between operations  1.29 us (3%)
    pallas_call x1, Pallas kernels, body(): pl.pallas_call(functools.partial(main_kernel, gz, pa), out_shape=(shape(3...  39.5 us
    pallas_call x1, Pallas kernels, body(): pl.pallas_call(functools.partial(finish_kernel, gz, pa, flat), out_shape=...  2.62 us

profile of v2, /device:TPU:1, one launch (start us, length us, event | category | flops | bytes accessed | tf_op | source)
XLA Modules:
  0.0 43.4 jit_solution(17130470406111855215)
XLA Ops:
  1.3 39.5 %step.1 = (f32[3,192,128]{2,1,0:T(8,128)}, f32[4,192,128]{2,1,0:T(8,128)}, f32[8,16,384]{2,1,0:T(8,128)}, f32[8,8,384]{2,1,0:T(8,128)}) custom-call(s32[1]{0:T(128)S(6)} %copy.14.counts, s32[1,1024]{1,0:T(1,128)} %bitcast.11, s32[1,1024]{1,0:T(1,128)} %bitcast.12, f32[16,1024]{1,0:T(8,128)} %bitcast.10, f32[3,192,128]{2,1,0:T(8,128)} %bitcast.9, ...), custom_call_target="tpu_custom_call" | custom-call | tf_op jit(solution)/shard_map/step/pallas_call | solution.py:451
  40.7 2.6 %finish.1 = (f32[3,192,128]{2,1,0:T(8,128)}, f32[16,3072]{1,0:T(8,128)}) custom-call(s32[1]{0:T(128)} %bitcast.where, f32[4,192,128]{2,1,0:T(8,128)} %get-tuple-element.8.hat, f32[3,192,128]{2,1,0:T(8,128)} %get-tuple-element.9.ustar, bf16[4,2,512,128]{3,2,1,0:T(8,128)(2,1)} %constant.17.clone.high, bf16[4,2,512,128]{3,2,1,0:T(8,128)(2,1)} %constant.18.clone.low, ...), custom_call_target="tpu_custom_call" | custom-call | tf_op jit(solution)/shard_map/finish/pallas_call | solution.py:472

commit v3 on v2

--- a/solution.py
+++ b/solution.py
@@ -197,7 +197,7 @@
     return out + jnp.dot(top, high, preferred_element_type=f32)
 
 
-def momentum(pa, speeds, viscosity, above, below, edge_left, edge_right, deposit, high, low, ustar, partial):
+def momentum(pa, speeds, viscosity, near, far, far_ready, edge_left, edge_right, deposit, high, low, ustar, partial):
     columns = speeds.shape[2]
     radius = radii()
     arc = 1.0 / (radius * (2.0 * math.pi / NTH)) ** 2
@@ -218,21 +218,23 @@
         return jnp.where(lane == 0, edge_left[:, 4 + f:5 + f], pltpu.roll(x, 1, 1))
 
     weights = [
-        0.5 * (nu + above[3]),
-        0.5 * (nu + below[3]),
+        0.5 * (nu + near[3]),
         (radius + 0.5) / radius * 0.5 * (nu + outward(nu)),
         (radius - 0.5) / radius * 0.5 * (nu + inward(nu)),
         arc * 0.5 * (nu + ahead(nu, 3)),
         arc * 0.5 * (nu + behind(nu, 3)),
     ]
-    new = []
     for c in range(3):
         u = speeds[c]
-        sides = (above[c], below[c], outward(u), inward(u), ahead(u, c), behind(u, c))
+        sides = (near[c], outward(u), inward(u), ahead(u, c), behind(u, c))
         total = weights[0] * (sides[0] - u)
         for w, s in zip(weights[1:], sides[1:]):
             total = total + w * (s - u)
-        new.append(u + STEP * (total + deposit[c]))
+        ustar[c] = u + STEP * (total + deposit[c])
+    far_ready()
+    weight = (0.5 * STEP) * (nu + far[3])
+    new = [ustar[c] + weight * (far[c] - speeds[c]) for c in range(3)]
+    for c in range(3):
         ustar[c] = new[c]
     radial = new[1]
     flux = jnp.where(row == NR - 1, 0.0, (radius + 0.5) * 0.5 * (radial + outward(radial)))
@@ -240,14 +242,15 @@
     across = new[2] / (2.0 * (2.0 * math.pi / NTH) * radius)
     out = split_dot(jnp.concatenate([divergence, across], 1), high[...], low[...])
     for q in range(pa):
-        partial[q] = out[:, q * columns:(q + 1) * columns]
+        partial[q % 2, q // 2] = out[:, q * columns:(q + 1) * columns]
 
 
 def main_kernel(gz, pa, counts, rank_in, cell_in, parcels_in, velocity, viscosity, high_in, low_in, ratios,
                 ustar, hat, second_in, fluid,
                 rank, cell, parcels, speeds, nu, high, low, held, first, second, first_in,
-                above, below, edges, edge_left, edge_right, deposit, partial, came,
-                lsem, fsend, frecv, send, recv, zsend, zrecv, esend, erecv, rsend, rrecv, gsend, grecv):
+                near, far, edges, edge_left, edge_right, deposit, partial, came, rest,
+                lsem, fsend, frecv, send, recv, zsend, zrecv, wsend, wrecv, esend, erecv, psend, precv, rsend, rrecv,
+                gsend, grecv, hsend, hrecv):
     me = lax.axis_index("gz")
     mp = lax.axis_index("pa")
     columns = nu.shape[1]
@@ -287,24 +290,47 @@
 
     loop(1, gz, lambda o: first_copy(o).start())
 
-    def plane(source, target, part, i, to):
+    odd = lax.rem(me, 2)
+    mate = me + 1 - 2 * odd
+    stride = 2 - 4 * odd
+    beyond, behind = me + stride, me - stride
+    has_beyond = jnp.logical_and(beyond >= 0, beyond < gz)
+    has_behind = jnp.logical_and(behind >= 0, behind < gz)
+    half = NR // 2
+    spots = [(f, pl.ds(r, half)) for r in (0, half) for f in range(4)]
+
+    def trade(i):
+        f, rows = spots[i]
+        source = velocity.at[f, rows] if f < 3 else viscosity.at[0, rows]
         return pltpu.make_async_remote_copy(
-            src_ref=source, dst_ref=target.at[part], send_sem=zsend.at[i], recv_sem=zrecv.at[i],
-            device_id=(to, mp), device_id_type=MESH)
-
-    up, down = lax.rem(me + 1, gz), lax.rem(me + gz - 1, gz)
-    to_up = [plane(velocity, below, pl.ds(0, 3), 0, up), plane(viscosity, below, pl.ds(3, 1), 1, up)]
-    to_down = [plane(velocity, above, pl.ds(0, 3), 2, down), plane(viscosity, above, pl.ds(3, 1), 3, down)]
-
-    @pl.when(me < gz - 1)
-    def _():
-        for c in to_up:
-            c.start()
-
-    @pl.when(me > 0)
-    def _():
-        for c in to_down:
-            c.start()
+            src_ref=source, dst_ref=near.at[f, rows], send_sem=zsend.at[i], recv_sem=zrecv.at[i],
+            device_id=(mate, mp), device_id_type=MESH)
+
+    def hand_on(i):
+        f, rows = spots[i]
+        return pltpu.make_async_remote_copy(
+            src_ref=near.at[f, rows], dst_ref=far.at[f, rows], send_sem=wsend.at[i], recv_sem=wrecv.at[i],
+            device_id=(lax.rem(beyond + gz, gz), mp), device_id_type=MESH)
+
+    for i in range(8):
+        trade(i).start()
+
+    def pass_on(i):
+        trade(i).wait_recv()
+
+        @pl.when(has_beyond)
+        def _():
+            hand_on(i).start()
+
+    def far_ready():
+        @pl.when(has_behind)
+        def _():
+            for i in range(8):
+                hand_on(i).wait_recv()
+
+        @pl.when(jnp.logical_not(has_behind))
+        def _():
+            far[...] = jnp.zeros_like(far)
 
     pieces, ends = [], []
     for c in range(3):
@@ -323,7 +349,6 @@
     ]
     for c in sides:
         c.start()
-    loop(1, gz, lambda o: second_copy(o).start())
     turned = jnp.concatenate(pieces, 0)
     deposit[...] = jnp.zeros_like(deposit)
     first_in[me] = first[me]
@@ -334,48 +359,44 @@
         first_copy(o).wait()
         deposit_slab(lax.rem(me + gz - o, gz), first_in, turned, fluid, deposit)
 
-    loop(1, gz, take)
+    done = 1
+    for i in range(8):
+        upto = 1 + (i + 1) * (gz - 1) // 8
+        loop(done, upto, take)
+        done = upto
+        pass_on(i)
     for c in sides:
         c.wait()
     for c in loads[5:]:
         c.wait()
-
-    @pl.when(me < gz - 1)
-    def _():
-        for c in to_up:
-            c.wait_send()
-        for c in to_down:
-            c.wait_recv()
-
-    @pl.when(me == gz - 1)
-    def _():
-        above[...] = jnp.zeros_like(above)
-
-    @pl.when(me > 0)
-    def _():
-        for c in to_down:
-            c.wait_send()
-        for c in to_up:
-            c.wait_recv()
-
-    @pl.when(me == 0)
-    def _():
-        below[...] = jnp.zeros_like(below)
-
-    momentum(pa, speeds, nu, above, below, edge_left[...].T, edge_right[...].T, deposit, high, low, ustar, partial)
-    sums = [
+    momentum(pa, speeds, nu, near, far, far_ready, edge_left[...].T, edge_right[...].T, deposit, high, low, ustar, partial)
+    core = lax.rem(mp, 2)
+    pair = mp + 1 - 2 * core
+    place = mp // 2
+    pairs = pa // 2
+    order = [lax.rem(place + 1 + i, pairs) for i in range(pairs)]
+    inner = [
         pltpu.make_async_remote_copy(
-            src_ref=partial.at[q], dst_ref=came.at[i], send_sem=rsend.at[i], recv_sem=rrecv.at[i],
-            device_id=(me, q), device_id_type=MESH)
-        for i, q in enumerate(others)
+            src_ref=partial.at[1 - core, q], dst_ref=came.at[q], send_sem=psend.at[i], recv_sem=precv.at[i],
+            device_id=(me, pair), device_id_type=MESH)
+        for i, q in enumerate(order)
     ]
-    for c in sums:
+    for c in inner:
         c.start()
-    for c in sums:
+    outer = []
+    for i, q in enumerate(order[:-1]):
+        inner[i].wait_recv()
+        came[q] = came[q] + partial[core, q]
+        outer.append(pltpu.make_async_remote_copy(
+            src_ref=came.at[q], dst_ref=rest.at[i], send_sem=rsend.at[i], recv_sem=rrecv.at[i],
+            device_id=(me, 2 * q + core), device_id_type=MESH))
+        outer[-1].start()
+    loop(1, gz, lambda o: second_copy(o).start())
+    inner[-1].wait_recv()
+    x = partial[core, place] + came[place]
+    for i, c in enumerate(outer):
         c.wait()
-    x = partial[mp]
-    for i in range(pa - 1):
-        x = x + came[i]
+        x = x + rest[i]
     radius = radii()
     mean = jnp.sum(radius * x, axis=0, keepdims=True) * (1.0 / (NR * (NR + NR / 2)))
     x = x - jnp.where(iota((1, columns), 1) + mp * columns == 0, mean, 0.0)
@@ -391,12 +412,31 @@
         pltpu.make_async_remote_copy(
             src_ref=hat.at[mp], dst_ref=hat.at[mp], send_sem=gsend.at[i], recv_sem=grecv.at[i],
             device_id=(me, q), device_id_type=MESH)
-        for i, q in enumerate(others)
+        for i, q in enumerate([2 * q + core for q in order[:-1]] + [pair])
     ]
     for c in spread:
         c.start()
-    for c in spread:
+    again = []
+    for i in range(pairs - 1):
+        q = 2 * lax.rem(place + 2 * pairs - 1 - i, pairs) + core
+        spread[i].wait_recv()
+        again.append(pltpu.make_async_remote_copy(
+            src_ref=hat.at[q], dst_ref=hat.at[q], send_sem=hsend.at[i], recv_sem=hrecv.at[i],
+            device_id=(me, pair), device_id_type=MESH))
+        again[-1].start()
+    spread[-1].wait_recv()
+    for c in again:
         c.wait()
+    for c in spread + inner:
+        c.wait_send()
+    for i in range(8):
+        trade(i).wait_send()
+
+    @pl.when(has_beyond)
+    def _():
+        for i in range(8):
+            hand_on(i).wait_send()
+
     loop(1, gz, lambda o: second_copy(o).wait())
 
 
@@ -459,9 +499,10 @@
             pltpu.VMEM((2 * columns, NTH), bf16), pltpu.VMEM((2 * columns, NTH), bf16), hold(*ratios.shape[1:]),
             hold(gz, 8, capacity), hold(gz, 16, capacity), hold(gz, 8, capacity),
             hold(4, NR, columns), hold(4, NR, columns), hold(8, NR), hold(8, NR), hold(8, NR),
-            hold(3, NR, columns), hold(pa, NR, columns), hold(pa - 1, NR, columns),
-            dma((8,)), dma((gz,)), dma((gz,)), dma((gz,)), dma((gz,)), dma((4,)), dma((4,)), dma((2,)), dma((2,)),
-            dma((pa - 1,)), dma((pa - 1,)), dma((pa - 1,)), dma((pa - 1,)),
+            hold(3, NR, columns), hold(2, pa // 2, NR, columns), hold(pa // 2, NR, columns), hold(pa // 2 - 1, NR, columns),
+            dma((8,)), dma((gz,)), dma((gz,)), dma((gz,)), dma((gz,)), dma((8,)), dma((8,)), dma((8,)), dma((8,)),
+            dma((2,)), dma((2,)), dma((pa // 2,)), dma((pa // 2,)), dma((pa // 2 - 1,)), dma((pa // 2 - 1,)),
+            dma((pa // 2,)), dma((pa // 2,)), dma((pa // 2 - 1,)), dma((pa // 2 - 1,)),
         ],
         compiler_params=pltpu.CompilerParams(collective_id=0, has_side_effects=True, vmem_limit_bytes=LIMIT),
         name="step",

time: 43.5 us -> 34.7 us (0.80)
  the two profiles are of different devices: /device:TPU:1 before, /device:TPU:5 now
where the time goes in v3:
time: 34.7 us; the launch traced here: 34.5 us
  Pallas kernels  33.2 us (96%)
  between operations  1.29 us (4%)
    pallas_call x1, Pallas kernels, body(): pl.pallas_call(functools.partial(main_kernel, gz, pa), out_shape=(shape(3...  30.6 us
    pallas_call x1, Pallas kernels, body(): pl.pallas_call(functools.partial(finish_kernel, gz, pa, flat), out_shape=...  2.62 us

profile of v3, /device:TPU:5, one launch (start us, length us, event | category | flops | bytes accessed | tf_op | source)
XLA Modules:
  0.0 34.5 jit_solution(10862723692296358713)
XLA Ops:
  1.3 30.6 %step.1 = (f32[3,192,128]{2,1,0:T(8,128)}, f32[4,192,128]{2,1,0:T(8,128)}, f32[8,16,384]{2,1,0:T(8,128)}, f32[8,8,384]{2,1,0:T(8,128)}) custom-call(s32[1]{0:T(128)S(6)} %copy.14.counts, s32[1,1024]{1,0:T(1,128)} %bitcast.11, s32[1,1024]{1,0:T(1,128)} %bitcast.12, f32[16,1024]{1,0:T(8,128)} %bitcast.10, f32[3,192,128]{2,1,0:T(8,128)} %bitcast.9, ...), custom_call_target="tpu_custom_call" | custom-call | tf_op jit(solution)/shard_map/step/pallas_call | solution.py:491
  31.9 2.6 %finish.1 = (f32[3,192,128]{2,1,0:T(8,128)}, f32[16,3072]{1,0:T(8,128)}) custom-call(s32[1]{0:T(128)} %bitcast.where, f32[4,192,128]{2,1,0:T(8,128)} %get-tuple-element.8.hat, f32[3,192,128]{2,1,0:T(8,128)} %get-tuple-element.9.ustar, bf16[4,2,512,128]{3,2,1,0:T(8,128)(2,1)} %constant.17.clone.high, bf16[4,2,512,128]{3,2,1,0:T(8,128)(2,1)} %constant.18.clone.low, ...), custom_call_target="tpu_custom_call" | custom-call | tf_op jit(solution)/shard_map/finish/pallas_call | solution.py:513

commit v4 on v3

--- a/solution.py
+++ b/solution.py
@@ -197,49 +197,55 @@
     return out + jnp.dot(top, high, preferred_element_type=f32)
 
 
-def momentum(pa, speeds, viscosity, near, far, far_ready, edge_left, edge_right, deposit, high, low, ustar, partial):
-    columns = speeds.shape[2]
+def face_weights(viscosity, near, edge_left, edge_right):
     radius = radii()
     arc = 1.0 / (radius * (2.0 * math.pi / NTH)) ** 2
     nu = viscosity[...]
-    row = iota((NR, columns), 0)
-    lane = iota((NR, columns), 1)
-
-    def outward(x):
-        return jnp.concatenate([x[1:], jnp.zeros_like(x[:1])], 0)
-
-    def inward(x):
-        return jnp.concatenate([jnp.zeros_like(x[:1]), x[:-1]], 0)
-
-    def ahead(x, f):
-        return jnp.where(lane == columns - 1, edge_right[:, f:f + 1], pltpu.roll(x, columns - 1, 1))
-
-    def behind(x, f):
-        return jnp.where(lane == 0, edge_left[:, 4 + f:5 + f], pltpu.roll(x, 1, 1))
-
-    weights = [
+    return [
         0.5 * (nu + near[3]),
         (radius + 0.5) / radius * 0.5 * (nu + outward(nu)),
         (radius - 0.5) / radius * 0.5 * (nu + inward(nu)),
-        arc * 0.5 * (nu + ahead(nu, 3)),
-        arc * 0.5 * (nu + behind(nu, 3)),
+        arc * 0.5 * (nu + ahead(nu, edge_right[:, 3:4])),
+        arc * 0.5 * (nu + behind(nu, edge_left[:, 7:8])),
     ]
-    for c in range(3):
-        u = speeds[c]
-        sides = (near[c], outward(u), inward(u), ahead(u, c), behind(u, c))
-        total = weights[0] * (sides[0] - u)
-        for w, s in zip(weights[1:], sides[1:]):
-            total = total + w * (s - u)
-        ustar[c] = u + STEP * (total + deposit[c])
-    far_ready()
-    weight = (0.5 * STEP) * (nu + far[3])
-    new = [ustar[c] + weight * (far[c] - speeds[c]) for c in range(3)]
-    for c in range(3):
-        ustar[c] = new[c]
-    radial = new[1]
-    flux = jnp.where(row == NR - 1, 0.0, (radius + 0.5) * 0.5 * (radial + outward(radial)))
+
+
+def outward(x):
+    return jnp.concatenate([x[1:], jnp.zeros_like(x[:1])], 0)
+
+
+def inward(x):
+    return jnp.concatenate([jnp.zeros_like(x[:1]), x[:-1]], 0)
+
+
+def ahead(x, edge):
+    columns = x.shape[1]
+    return jnp.where(iota(x.shape, 1) == columns - 1, edge, pltpu.roll(x, columns - 1, 1))
+
+
+def behind(x, edge):
+    return jnp.where(iota(x.shape, 1) == 0, edge, pltpu.roll(x, 1, 1))
+
+
+def most_of(c, speeds, near, edge_left, edge_right, deposit, weights):
+    u = speeds[c]
+    sides = (near[c], outward(u), inward(u), ahead(u, edge_right[:, c:c + 1]), behind(u, edge_left[:, 4 + c:5 + c]))
+    total = deposit[c]
+    for w, s in zip(weights, sides):
+        total = total + w * (s - u)
+    return u + STEP * total
+
+
+def far_part(c, speeds, viscosity, far):
+    return (0.5 * STEP) * (viscosity[...] + far[3]) * (far[c] - speeds[c])
+
+
+def transform(pa, radial, azimuthal, high, low, partial):
+    columns = radial.shape[1]
+    radius = radii()
+    flux = jnp.where(iota(radial.shape, 0) == NR - 1, 0.0, (radius + 0.5) * 0.5 * (radial + outward(radial)))
     divergence = (flux - inward(flux)) / radius
-    across = new[2] / (2.0 * (2.0 * math.pi / NTH) * radius)
+    across = azimuthal / (2.0 * (2.0 * math.pi / NTH) * radius)
     out = split_dot(jnp.concatenate([divergence, across], 1), high[...], low[...])
     for q in range(pa):
         partial[q % 2, q // 2] = out[:, q * columns:(q + 1) * columns]
@@ -271,10 +277,6 @@
     others = [lax.rem(mp + o, pa) for o in range(1, pa)]
     for q in others:
         pl.semaphore_signal(barrier, inc=1, device_id=(me, q), device_id_type=MESH)
-    for c in loads[:5]:
-        c.wait()
-    pack(gz, counts, rank, cell, parcels, first, second)
-    pl.semaphore_wait(barrier, gz + pa - 2)
 
     def slab_copy(source, target, ssem, rsem, o):
         to = lax.rem(me + o, gz)
@@ -288,16 +290,14 @@
     def second_copy(o):
         return slab_copy(second, second_in, send, recv, o)
 
-    loop(1, gz, lambda o: first_copy(o).start())
-
     odd = lax.rem(me, 2)
     mate = me + 1 - 2 * odd
     stride = 2 - 4 * odd
-    beyond, behind = me + stride, me - stride
+    beyond, before = me + stride, me - stride
     has_beyond = jnp.logical_and(beyond >= 0, beyond < gz)
-    has_behind = jnp.logical_and(behind >= 0, behind < gz)
+    has_before = jnp.logical_and(before >= 0, before < gz)
     half = NR // 2
-    spots = [(f, pl.ds(r, half)) for r in (0, half) for f in range(4)]
+    spots = [(f, pl.ds(r, half)) for r in (0, half) for f in (3, 1, 2)] + [(0, pl.ds(r, half)) for r in (0, half)]
 
     def trade(i):
         f, rows = spots[i]
@@ -312,7 +312,18 @@
             src_ref=near.at[f, rows], dst_ref=far.at[f, rows], send_sem=wsend.at[i], recv_sem=wrecv.at[i],
             device_id=(lax.rem(beyond + gz, gz), mp), device_id_type=MESH)
 
-    for i in range(8):
+    @pl.when(jnp.logical_not(has_before))
+    def _():
+        far[...] = jnp.zeros_like(far)
+
+    pl.semaphore_wait(barrier, gz + pa - 2)
+    for i in range(3):
+        trade(i).start()
+    for c in loads[:5]:
+        c.wait()
+    pack(gz, counts, rank, cell, parcels, first, second)
+    loop(1, gz, lambda o: first_copy(o).start())
+    for i in range(3, 6):
         trade(i).start()
 
     def pass_on(i):
@@ -322,15 +333,11 @@
         def _():
             hand_on(i).start()
 
-    def far_ready():
-        @pl.when(has_behind)
+    def far_ready(numbers):
+        @pl.when(has_before)
         def _():
-            for i in range(8):
+            for i in numbers:
                 hand_on(i).wait_recv()
-
-        @pl.when(jnp.logical_not(has_behind))
-        def _():
-            far[...] = jnp.zeros_like(far)
 
     pieces, ends = [], []
     for c in range(3):
@@ -349,6 +356,8 @@
     ]
     for c in sides:
         c.start()
+    for i in range(6, 8):
+        trade(i).start()
     turned = jnp.concatenate(pieces, 0)
     deposit[...] = jnp.zeros_like(deposit)
     first_in[me] = first[me]
@@ -360,8 +369,8 @@
         deposit_slab(lax.rem(me + gz - o, gz), first_in, turned, fluid, deposit)
 
     done = 1
-    for i in range(8):
-        upto = 1 + (i + 1) * (gz - 1) // 8
+    for i in range(6):
+        upto = 1 + (i + 1) * (gz - 1) // 6
         loop(done, upto, take)
         done = upto
         pass_on(i)
@@ -369,7 +378,15 @@
         c.wait()
     for c in loads[5:]:
         c.wait()
-    momentum(pa, speeds, nu, near, far, far_ready, edge_left[...].T, edge_right[...].T, deposit, high, low, ustar, partial)
+    edge_l, edge_r = edge_left[...].T, edge_right[...].T
+    weights = face_weights(nu, near, edge_l, edge_r)
+    for c in (1, 2):
+        ustar[c] = most_of(c, speeds, near, edge_l, edge_r, deposit, weights)
+    far_ready(range(6))
+    radial, azimuthal = [ustar[c] + far_part(c, speeds, nu, far) for c in (1, 2)]
+    ustar[1] = radial
+    ustar[2] = azimuthal
+    transform(pa, radial, azimuthal, high, low, partial)
     core = lax.rem(mp, 2)
     pair = mp + 1 - 2 * core
     place = mp // 2
@@ -391,7 +408,11 @@
             src_ref=came.at[q], dst_ref=rest.at[i], send_sem=rsend.at[i], recv_sem=rrecv.at[i],
             device_id=(me, 2 * q + core), device_id_type=MESH))
         outer[-1].start()
+    for i in (6, 7):
+        pass_on(i)
     loop(1, gz, lambda o: second_copy(o).start())
+    weights = face_weights(nu, near, edge_l, edge_r)
+    ustar[0] = most_of(0, speeds, near, edge_l, edge_r, deposit, weights)
     inner[-1].wait_recv()
     x = partial[core, place] + came[place]
     for i, c in enumerate(outer):
@@ -416,6 +437,8 @@
     ]
     for c in spread:
         c.start()
+    far_ready((6, 7))
+    ustar[0] = ustar[0] + far_part(0, speeds, nu, far)
     again = []
     for i in range(pairs - 1):
         q = 2 * lax.rem(place + 2 * pairs - 1 - i, pairs) + core
@@ -483,7 +506,7 @@
     where = lax.axis_index("pa").astype(jnp.int32).reshape(1)
     high, low = forward_table(pa)
     ratios = radial_ratios(pa)
-    ANY = pl.BlockSpec(memory_space=pl.ANY)
+    ANY = pl.BlockSpec(memory_space=pltpu.HBM)
 
     def hold(*s):
         return pltpu.VMEM(s, f32)

time: 34.7 us -> 34.8 us (level)
  no operation moved by 1% of the time
where the time goes in v4:
time: 34.8 us; the launch traced here: 34.6 us
  Pallas kernels  33.3 us (96%)
  between operations  1.29 us (4%)
    pallas_call x1, Pallas kernels, body(): pl.pallas_call(functools.partial(main_kernel, gz, pa), out_shape=(shape(3...  30.7 us
    pallas_call x1, Pallas kernels, body(): pl.pallas_call(functools.partial(finish_kernel, gz, pa, flat), out_shape=...  2.62 us

profile of v4, /device:TPU:5, one launch (start us, length us, event | category | flops | bytes accessed | tf_op | source)
XLA Modules:
  0.0 34.6 jit_solution(11816162157494996484)
XLA Ops:
  1.3 30.7 %step.1 = (f32[3,192,128]{2,1,0:T(8,128)}, f32[4,192,128]{2,1,0:T(8,128)}, f32[8,16,384]{2,1,0:T(8,128)}, f32[8,8,384]{2,1,0:T(8,128)}) custom-call(s32[1]{0:T(128)S(6)} %copy.14.counts, s32[1,1024]{1,0:T(1,128)} %bitcast.11, s32[1,1024]{1,0:T(1,128)} %bitcast.12, f32[16,1024]{1,0:T(8,128)} %bitcast.10, f32[3,192,128]{2,1,0:T(8,128)} %bitcast.9, ...), custom_call_target="tpu_custom_call" | custom-call | tf_op jit(solution)/shard_map/step/pallas_call | solution.py:514
  32.0 2.6 %finish.1 = (f32[3,192,128]{2,1,0:T(8,128)}, f32[16,3072]{1,0:T(8,128)}) custom-call(s32[1]{0:T(128)} %bitcast.where, f32[4,192,128]{2,1,0:T(8,128)} %get-tuple-element.8.hat, f32[3,192,128]{2,1,0:T(8,128)} %get-tuple-element.9.ustar, bf16[4,2,512,128]{3,2,1,0:T(8,128)(2,1)} %constant.17.clone.high, bf16[4,2,512,128]{3,2,1,0:T(8,128)(2,1)} %constant.18.clone.low, ...), custom_call_target="tpu_custom_call" | custom-call | tf_op jit(solution)/shard_map/finish/pallas_call | solution.py:536

commit v5 on v4

--- a/solution.py
+++ b/solution.py
@@ -117,10 +117,14 @@
         lax.fori_loop(first, last, lambda i, _: (step(i), 0)[1], 0)
 
 
-def pack(gz, counts, rank, cell, parcels, first, second):
+def thirds(x):
+    one = x.astype(bf16).astype(f32)
+    two = (x - one).astype(bf16).astype(f32)
+    return [one, two, x - one - two]
+
+
+def slots_of(gz, capacity, counts, rank):
     block = rank.shape[1]
-    capacity = first.shape[2]
-    tiles = capacity // 128
     live = iota((1, block), 1) < counts[0]
     target = jnp.where(live, rank[...], gz)
     marks = (iota((gz, block), 0) == target).astype(f32)
@@ -134,39 +138,50 @@
         carry = carry + jnp.sum(part, axis=1, keepdims=True)
     slot = jnp.concatenate(slots, 1).astype(jnp.int32)
     place = jnp.where(live, target * capacity + slot, -1)
-    high = place >> 7
-    low = place & 127
-    low_hot = (iota((128, block), 0) == low).astype(f32).astype(bf16)
-    values = parcels[...]
-    one = values.astype(bf16).astype(f32)
-    two = (values - one).astype(bf16).astype(f32)
-    three = values - one - two
-    cells = cell[...]
-    line = ((cells >> 7) + 1).astype(f32)
-    column = (cells & 127).astype(f32)
-    table = jnp.concatenate([one, two, three, line, column, jnp.zeros((14, block), f32)], 0)
+    low_hot = (iota((128, block), 0) == (place & 127)).astype(f32).astype(bf16)
+    return place >> 7, low_hot
+
+
+def place_rows(gz, high, low_hot, table, target, combine):
+    height = table.shape[0]
+    tiles = target.shape[2] // 128
 
     def slab(g):
         left = [jnp.where(high == g * tiles + i, table, 0.0).astype(bf16) for i in range(tiles)]
         got = lax.dot_general(jnp.concatenate(left, 0), low_hot, (((1,), (1,)), ((), ())), preferred_element_type=f32)
         for i in range(tiles):
-            r = got[64 * i:64 * i + 64]
-            rows = r[0:16] + r[16:32] + r[32:48]
-            lanes = slice(128 * i, 128 * i + 128)
-            second[g, :, lanes] = rows
-            code = r[48:49] * 128.0 + r[49:50]
-            total = 0.0
-            for half in (rows[0:8], rows[8:16]):
-                is_rate, rate = rates_of(half)
-                weight = rate / (1.0 + STEP * rate)
-                total = total + jnp.where(is_rate, weight, weight * half)
-            total = total + rolled(total, 4)
-            first[g, :, lanes] = jnp.where(iota(total.shape, 0) == 4, code, total)
+            target[g, :, 128 * i:128 * i + 128] = combine(got[height * i:height * i + height])
 
     loop(0, gz, slab)
 
 
-def deposit_slab(g, came, turned, fluid, deposit):
+def drag_table(parcels, cell):
+    total = 0.0
+    for half in (parcels[0:8], parcels[8:16]):
+        is_rate, rate = rates_of(half)
+        weight = rate / (1.0 + STEP * rate)
+        total = total + jnp.where(is_rate, weight, weight * half)
+    total = total + rolled(total, 4)
+    first = iota(total.shape, 0) < 4
+    one, two, three = thirds(total)
+    cells = cell[...]
+    line = ((cells >> 7) + 1).astype(f32)
+    column = (cells & 127).astype(f32)
+    row = iota(total.shape, 0)
+    last = jnp.where(first, three, jnp.where(row == 4, line, jnp.where(row == 5, column, 0.0)))
+    return jnp.concatenate([jnp.where(first, one, two), last], 0)
+
+
+def drag_rows(r):
+    sums = r[0:8] + rolled(r[0:8], 4) + r[8:16]
+    return jnp.where(iota(sums.shape, 0) == 4, r[12:13] * 128.0 + r[13:14], sums)
+
+
+def parcel_rows(r):
+    return r[0:16] + r[16:32] + r[32:48]
+
+
+def deposit_slab(g, came, turned, fluid, deposit, parts):
     columns = deposit.shape[2]
     rows = came[g]
     capacity = rows.shape[1]
@@ -176,18 +191,17 @@
     line_hot = (iota((NR, capacity), 0) == line).astype(f32).astype(bf16)
     column_hot = iota((columns, capacity), 0) == column
     picked = jnp.dot(turned, line_hot, preferred_element_type=f32)
-    looked, pushes = [], []
-    for c in range(3):
-        both = picked[2 * c * columns:(2 * c + 1) * columns] + picked[(2 * c + 1) * columns:(2 * c + 2) * columns]
+    pushes = []
+    for i, c in enumerate(parts):
+        both = picked[2 * i * columns:(2 * i + 1) * columns] + picked[(2 * i + 1) * columns:(2 * i + 2) * columns]
         speed = jnp.sum(jnp.where(column_hot, both, 0.0), axis=0, keepdims=True)
         drag = (rows[c:c + 1] - speed * rows[3:4]).astype(bf16).astype(f32)
-        looked.append(speed)
+        fluid[g, c:c + 1] = speed
+        fluid[g, 4 + c:5 + c] = speed
         pushes.append(jnp.where(column_hot, drag, 0.0).astype(bf16))
-    nothing = jnp.zeros_like(looked[0])
-    fluid[g] = jnp.concatenate((looked + [nothing]) * 2, 0)
     added = lax.dot_general(line_hot, jnp.concatenate(pushes, 0), (((1,), (1,)), ((), ())), preferred_element_type=f32)
-    for c in range(3):
-        deposit[c] += added[:, c * columns:(c + 1) * columns]
+    for i, c in enumerate(parts):
+        deposit[c] += added[:, i * columns:(i + 1) * columns]
 
 
 def split_dot(x, high, low):
@@ -278,8 +292,15 @@
     for q in others:
         pl.semaphore_signal(barrier, inc=1, device_id=(me, q), device_id_type=MESH)
 
+    def peer(o):
+        to, bit = 0, 1
+        while bit < gz:
+            to = to + bit * lax.rem(me // bit + o // bit, 2)
+            bit = bit * 2
+        return to
+
     def slab_copy(source, target, ssem, rsem, o):
-        to = lax.rem(me + o, gz)
+        to = peer(o)
         return pltpu.make_async_remote_copy(
             src_ref=source.at[to], dst_ref=target.at[me], send_sem=ssem.at[o], recv_sem=rsem.at[o],
             device_id=(to, mp), device_id_type=MESH)
@@ -321,8 +342,10 @@
         trade(i).start()
     for c in loads[:5]:
         c.wait()
-    pack(gz, counts, rank, cell, parcels, first, second)
-    loop(1, gz, lambda o: first_copy(o).start())
+    high_part, low_hot = slots_of(gz, first.shape[2], counts, rank)
+    values = parcels[...]
+    place_rows(gz, high_part, low_hot, drag_table(values, cell), first, drag_rows)
+    loop(1, gz, lambda o: first_copy(gz - o).start())
     for i in range(3, 6):
         trade(i).start()
 
@@ -358,15 +381,18 @@
         c.start()
     for i in range(6, 8):
         trade(i).start()
-    turned = jnp.concatenate(pieces, 0)
+    place_rows(gz, high_part, low_hot, jnp.concatenate(thirds(values), 0), second, parcel_rows)
+    turned = jnp.concatenate(pieces[2:], 0)
+    turned_axial = jnp.concatenate(pieces[:2], 0)
+    fluid[...] = jnp.zeros_like(fluid)
     deposit[...] = jnp.zeros_like(deposit)
     first_in[me] = first[me]
     second_in[me] = second[me]
-    deposit_slab(me, first_in, turned, fluid, deposit)
+    deposit_slab(me, first_in, turned, fluid, deposit, (1, 2))
 
     def take(o):
         first_copy(o).wait()
-        deposit_slab(lax.rem(me + gz - o, gz), first_in, turned, fluid, deposit)
+        deposit_slab(peer(o), first_in, turned, fluid, deposit, (1, 2))
 
     done = 1
     for i in range(6):
@@ -410,9 +436,12 @@
         outer[-1].start()
     for i in (6, 7):
         pass_on(i)
-    loop(1, gz, lambda o: second_copy(o).start())
-    weights = face_weights(nu, near, edge_l, edge_r)
-    ustar[0] = most_of(0, speeds, near, edge_l, edge_r, deposit, weights)
+    loop(1, gz, lambda o: second_copy(gz - o).start())
+
+    def axial(o):
+        deposit_slab(peer(o), first_in, turned_axial, fluid, deposit, (0,))
+
+    loop(0, gz // 2, axial)
     inner[-1].wait_recv()
     x = partial[core, place] + came[place]
     for i, c in enumerate(outer):
@@ -437,8 +466,6 @@
     ]
     for c in spread:
         c.start()
-    far_ready((6, 7))
-    ustar[0] = ustar[0] + far_part(0, speeds, nu, far)
     again = []
     for i in range(pairs - 1):
         q = 2 * lax.rem(place + 2 * pairs - 1 - i, pairs) + core
@@ -447,6 +474,11 @@
             src_ref=hat.at[q], dst_ref=hat.at[q], send_sem=hsend.at[i], recv_sem=hrecv.at[i],
             device_id=(me, pair), device_id_type=MESH))
         again[-1].start()
+    loop(gz // 2, gz, axial)
+    weights = face_weights(nu, near, edge_l, edge_r)
+    ustar[0] = most_of(0, speeds, near, edge_l, edge_r, deposit, weights)
+    far_ready((6, 7))
+    ustar[0] = ustar[0] + far_part(0, speeds, nu, far)
     spread[-1].wait_recv()
     for c in again:
         c.wait()

time: 34.8 us -> 34.1 us (0.980)
  the two profiles are of different devices: /device:TPU:5 before, /device:TPU:1 now
where the time goes in v5:
time: 34.1 us; the launch traced here: 33.6 us
  Pallas kernels  32.4 us (95%)
  between operations  1.29 us (4%)
    pallas_call x1, Pallas kernels, body(): pl.pallas_call(functools.partial(main_kernel, gz, pa), out_shape=(shape(3...  29.7 us
    pallas_call x1, Pallas kernels, body(): pl.pallas_call(functools.partial(finish_kernel, gz, pa, flat), out_shape=...  2.62 us

profile of v5, /device:TPU:1, one launch (start us, length us, event | category | flops | bytes accessed | tf_op | source)
XLA Modules:
  0.0 33.6 jit_solution(7802071118947100564)
XLA Ops:
  1.3 29.7 %step.1 = (f32[3,192,128]{2,1,0:T(8,128)}, f32[4,192,128]{2,1,0:T(8,128)}, f32[8,16,384]{2,1,0:T(8,128)}, f32[8,8,384]{2,1,0:T(8,128)}) custom-call(s32[1]{0:T(128)S(6)} %copy.14.counts, s32[1,1024]{1,0:T(1,128)} %bitcast.11, s32[1,1024]{1,0:T(1,128)} %bitcast.12, f32[16,1024]{1,0:T(8,128)} %bitcast.10, f32[3,192,128]{2,1,0:T(8,128)} %bitcast.9, ...), custom_call_target="tpu_custom_call" | custom-call | tf_op jit(solution)/shard_map/step/pallas_call | solution.py:546
  31.0 2.6 %finish.1 = (f32[3,192,128]{2,1,0:T(8,128)}, f32[16,3072]{1,0:T(8,128)}) custom-call(s32[1]{0:T(128)} %bitcast.where, f32[4,192,128]{2,1,0:T(8,128)} %get-tuple-element.8.hat, f32[3,192,128]{2,1,0:T(8,128)} %get-tuple-element.9.ustar, bf16[4,2,512,128]{3,2,1,0:T(8,128)(2,1)} %constant.17.clone.high, bf16[4,2,512,128]{3,2,1,0:T(8,128)(2,1)} %constant.18.clone.low, ...), custom_call_target="tpu_custom_call" | custom-call | tf_op jit(solution)/shard_map/finish/pallas_call | solution.py:568

commit v6 on v5

--- a/solution.py
+++ b/solution.py
@@ -53,7 +53,7 @@
     parts = []
     for p in range(pa):
         part = slice(p * columns, (p + 1) * columns)
-        parts.append(np.stack([same[:, part], beside[:, part]]))
+        parts.append(np.stack([same[:, part], beside[:, part]]).reshape(2, pa, columns, columns))
     return halves(np.stack(parts))
 
 
@@ -265,9 +265,9 @@
         partial[q % 2, q // 2] = out[:, q * columns:(q + 1) * columns]
 
 
-def main_kernel(gz, pa, counts, rank_in, cell_in, parcels_in, velocity, viscosity, high_in, low_in, ratios,
-                ustar, hat, second_in, fluid,
-                rank, cell, parcels, speeds, nu, high, low, held, first, second, first_in,
+def main_kernel(gz, pa, flat, counts, rank_in, cell_in, parcels_in, velocity, viscosity, high_in, low_in, ratios,
+                high_back, low_back, velocity_out, parcels_out,
+                ustar, hat, second_in, fluid, back_high, back_low, rank, cell, parcels, speeds, nu, high, low, held, first, second, first_in,
                 near, far, edges, edge_left, edge_right, deposit, partial, came, rest,
                 lsem, fsend, frecv, send, recv, zsend, zrecv, wsend, wrecv, esend, erecv, psend, precv, rsend, rrecv,
                 gsend, grecv, hsend, hrecv):
@@ -278,7 +278,8 @@
         pltpu.make_async_copy(a, b, lsem.at[i])
         for i, (a, b) in enumerate((
             (rank_in, rank), (cell_in, cell), (parcels_in, parcels), (velocity, speeds), (viscosity.at[0], nu),
-            (high_in.at[mp], high), (low_in.at[mp], low), (ratios.at[mp], held)))
+            (high_in.at[mp], high), (low_in.at[mp], low), (ratios.at[mp], held),
+            (high_back.at[mp], back_high), (low_back.at[mp], back_low)))
     ]
     for c in loads:
         c.start()
@@ -400,6 +401,7 @@
         loop(done, upto, take)
         done = upto
         pass_on(i)
+    loop(1, gz, lambda o: second_copy(gz - o).start())
     for c in sides:
         c.wait()
     for c in loads[5:]:
@@ -436,7 +438,6 @@
         outer[-1].start()
     for i in (6, 7):
         pass_on(i)
-    loop(1, gz, lambda o: second_copy(gz - o).start())
 
     def axial(o):
         deposit_slab(peer(o), first_in, turned_axial, fluid, deposit, (0,))
@@ -466,22 +467,37 @@
     ]
     for c in spread:
         c.start()
-    again = []
+
+    def back(q, sums):
+        block = hat[q]
+        slope = 0.5 * (jnp.concatenate([block[1:], block[-1:]], 0) - jnp.concatenate([block[:1], block[:-1]], 0))
+        return (sums[0] + split_dot(slope, back_high[0, q], back_low[0, q]),
+                sums[1] + split_dot(block, back_high[1, q], back_low[1, q]))
+
+    grads = back(mp, (0.0, 0.0))
+    loop(gz // 2, gz, axial)
+    spread[-1].wait_recv()
+    grads = back(2 * place + 1 - core, grads)
+    again, froms = [], []
     for i in range(pairs - 1):
-        q = 2 * lax.rem(place + 2 * pairs - 1 - i, pairs) + core
+        froms.append(2 * lax.rem(place + 2 * pairs - 1 - i, pairs))
+        q = froms[-1] + core
         spread[i].wait_recv()
         again.append(pltpu.make_async_remote_copy(
             src_ref=hat.at[q], dst_ref=hat.at[q], send_sem=hsend.at[i], recv_sem=hrecv.at[i],
             device_id=(me, pair), device_id_type=MESH))
         again[-1].start()
-    loop(gz // 2, gz, axial)
+    for q in froms:
+        grads = back(q + core, grads)
     weights = face_weights(nu, near, edge_l, edge_r)
-    ustar[0] = most_of(0, speeds, near, edge_l, edge_r, deposit, weights)
+    axial_speed = most_of(0, speeds, near, edge_l, edge_r, deposit, weights)
     far_ready((6, 7))
-    ustar[0] = ustar[0] + far_part(0, speeds, nu, far)
-    spread[-1].wait_recv()
-    for c in again:
-        c.wait()
+    velocity_out[0] = axial_speed + far_part(0, speeds, nu, far)
+    for i, q in enumerate(froms):
+        again[i].wait()
+        grads = back(q + 1 - core, grads)
+    velocity_out[1] = ustar[1] - grads[0]
+    velocity_out[2] = ustar[2] - grads[1] / (2.0 * (2.0 * math.pi / NTH) * radii())
     for c in spread + inner:
         c.wait_send()
     for i in range(8):
@@ -492,32 +508,28 @@
         for i in range(8):
             hand_on(i).wait_send()
 
-    loop(1, gz, lambda o: second_copy(o).wait())
-
-
-def finish_kernel(gz, pa, flat, where, hat, ustar, high, low, second, fluid, velocity_out, parcels_out):
-    capacity = second.shape[2]
-    x = jnp.concatenate([hat[q] for q in range(pa)], 1)
-    slope = 0.5 * (jnp.concatenate([x[1:], x[-1:]], 0) - jnp.concatenate([x[:1], x[:-1]], 0))
-    velocity_out[0] = ustar[0]
-    velocity_out[1] = ustar[1] - split_dot(slope, high[0, 0], low[0, 0])
-    turn = split_dot(x, high[0, 1], low[0, 1]) / (2.0 * (2.0 * math.pi / NTH) * radii())
-    velocity_out[2] = ustar[2] - turn
-
-    def slab(g, _):
-        speed = fluid[g]
-        for h in (0, 8):
-            rows = second[g, h:h + 8]
-            is_rate, rate = rates_of(rows)
-            moved = (rows + STEP * rate * speed) / (1.0 + STEP * rate)
-            rows = jnp.where(is_rate, rows, moved)
-            if flat:
-                parcels_out[h:h + 8, pl.ds(pl.multiple_of(g * capacity, 128), capacity)] = rows
-            else:
-                parcels_out[g, h:h + 8] = rows
-        return 0
-
-    lax.fori_loop(0, gz, slab, 0, unroll=gz <= 8)
+    def arrive(o):
+        g = peer(o)
+        if not (isinstance(o, int) and o == 0):
+            second_copy(o).wait()
+        rows = move_rows(second_in[g], fluid[g])
+        if flat:
+            capacity = rows.shape[1]
+            parcels_out[:, pl.ds(pl.multiple_of(g * capacity, 128), capacity)] = rows
+        else:
+            parcels_out[g] = rows
+
+    arrive(0)
+    loop(1, gz, arrive)
+
+
+def move_rows(rows, speed):
+    out = []
+    for h in (0, 8):
+        part = rows[h:h + 8]
+        is_rate, rate = rates_of(part)
+        out.append(jnp.where(is_rate, part, (part + STEP * rate * speed) / (1.0 + STEP * rate)))
+    return jnp.concatenate(out, 0)
 
 
 def body(velocity, viscosity, parcels, dest_rank, dest_cell, counts):
@@ -533,48 +545,37 @@
     def shape(*s):
         return jax.ShapeDtypeStruct(s, f32)
 
-    plain = pltpu.CompilerParams(vmem_limit_bytes=LIMIT)
     dma = pltpu.SemaphoreType.DMA
-    where = lax.axis_index("pa").astype(jnp.int32).reshape(1)
     high, low = forward_table(pa)
+    high_back, low_back = inverse_table(pa)
     ratios = radial_ratios(pa)
     ANY = pl.BlockSpec(memory_space=pltpu.HBM)
 
     def hold(*s):
         return pltpu.VMEM(s, f32)
 
-    ustar, hat, second, fluid = pl.pallas_call(
-        functools.partial(main_kernel, gz, pa),
-        out_shape=(shape(3, NR, columns), shape(pa, NR, columns), shape(gz, 16, capacity), shape(gz, 8, capacity)),
-        in_specs=[pl.BlockSpec(memory_space=pltpu.SMEM)] + [ANY] * 8,
-        out_specs=(VM,) * 4,
+    velocity_out, parcels_out = pl.pallas_call(
+        functools.partial(main_kernel, gz, pa, flat),
+        out_shape=(shape(3, NR, columns), shape(16, gz * slots) if flat else shape(gz, 16, capacity)),
+        in_specs=[pl.BlockSpec(memory_space=pltpu.SMEM)] + [ANY] * 10,
+        out_specs=(VM, VM),
         scratch_shapes=[
+            hold(3, NR, columns), hold(pa, NR, columns), hold(gz, 16, capacity), hold(gz, 8, capacity),
+            pltpu.VMEM((2, pa, columns, columns), bf16), pltpu.VMEM((2, pa, columns, columns), bf16),
             pltpu.VMEM((1, block), jnp.int32), pltpu.VMEM((1, block), jnp.int32), hold(16, block),
             hold(3, NR, columns), hold(NR, columns),
             pltpu.VMEM((2 * columns, NTH), bf16), pltpu.VMEM((2 * columns, NTH), bf16), hold(*ratios.shape[1:]),
             hold(gz, 8, capacity), hold(gz, 16, capacity), hold(gz, 8, capacity),
             hold(4, NR, columns), hold(4, NR, columns), hold(8, NR), hold(8, NR), hold(8, NR),
             hold(3, NR, columns), hold(2, pa // 2, NR, columns), hold(pa // 2, NR, columns), hold(pa // 2 - 1, NR, columns),
-            dma((8,)), dma((gz,)), dma((gz,)), dma((gz,)), dma((gz,)), dma((8,)), dma((8,)), dma((8,)), dma((8,)),
+            dma((10,)), dma((gz,)), dma((gz,)), dma((gz,)), dma((gz,)), dma((8,)), dma((8,)), dma((8,)), dma((8,)),
             dma((2,)), dma((2,)), dma((pa // 2,)), dma((pa // 2,)), dma((pa // 2 - 1,)), dma((pa // 2 - 1,)),
             dma((pa // 2,)), dma((pa // 2,)), dma((pa // 2 - 1,)), dma((pa // 2 - 1,)),
         ],
         compiler_params=pltpu.CompilerParams(collective_id=0, has_side_effects=True, vmem_limit_bytes=LIMIT),
         name="step",
     )(counts, dest_rank.reshape(1, block), dest_cell.reshape(1, block), parcels.T, velocity,
-      viscosity, high, low, ratios)
-    high, low = inverse_table(pa)
-    chosen = pl.BlockSpec((1, 2, NTH, columns), lambda i, w: (w[0], 0, 0, 0))
-    velocity_out, parcels_out = pl.pallas_call(
-        functools.partial(finish_kernel, gz, pa, flat),
-        out_shape=(shape(3, NR, columns), shape(16, gz * slots) if flat else shape(gz, 16, capacity)),
-        grid_spec=pltpu.PrefetchScalarGridSpec(
-            num_scalar_prefetch=1, grid=(1,),
-            in_specs=[VM, VM, chosen, chosen, VM, VM],
-            out_specs=(VM, VM)),
-        compiler_params=plain,
-        name="finish",
-    )(where, hat, ustar, high, low, second, fluid)
+      viscosity, high, low, ratios, high_back, low_back)
     if not flat:
         parcels_out = parcels_out[:, :, :slots].transpose(1, 0, 2).reshape(16, gz * slots)
     return velocity_out.reshape(3, 1, NR, columns), parcels_out.T

time: 34.1 us -> 36.8 us (1.079)
  the two profiles are of different devices: /device:TPU:1 before, /device:TPU:11 now
where the time goes in v6:
time: 36.8 us; the launch traced here: 36.6 us
  Pallas kernels  32 us (87%)
  local copies, waits for them, and re-layouts  3.31 us (9%)
  between operations  1.29 us (4%)
    pallas_call x1, Pallas kernels, body(): pl.pallas_call(functools.partial(main_kernel, gz, pa, flat), out_shape=(s...  32 us
    unnamed x2, local copies, waits for them, and re-layouts  3.31 us

profile of v6, /device:TPU:11, one launch (start us, length us, event | category | flops | bytes accessed | tf_op | source)
XLA Modules:
  0.0 36.6 jit_solution(13975771119323582015)
XLA Ops:
  1.3 32.0 %step.1 = (f32[3,192,128]{2,1,0:T(8,128)}, f32[16,3072]{1,0:T(8,128)}) custom-call(s32[1]{0:T(128)S(6)} %copy.16.counts, s32[1,1024]{1,0:T(1,128)} %bitcast.12, s32[1,1024]{1,0:T(1,128)} %bitcast.13, f32[16,1024]{1,0:T(8,128)} %bitcast.11, f32[3,192,128]{2,1,0:T(8,128)} %bitcast.8, f32[1,192,128]{2,1,0:T(8,128)} %viscosity.1, ...), custom_call_target="tpu_custom_call" | custom-call | tf_op jit(solution)/shard_map/step/pallas_call | solution.py:557
  33.3 1.7 %copy.17 = f32[3,1,192,128]{3,2,1,0:T(8,128)} copy(f32[3,1,192,128]{3,2,1,0:T(8,128)} %bitcast.9) | data formatting | bytes 589824
  35.0 1.6 %copy.18 = f32[3072,16]{0,1:T(8,128)} copy(f32[3072,16]{0,1:T(8,128)} %bitcast.10) | data formatting | bytes 393216

commit v7 on v5

--- a/solution.py
+++ b/solution.py
@@ -362,6 +362,8 @@
             for i in numbers:
                 hand_on(i).wait_recv()
 
+    for i in (0, 1):
+        pass_on(i)
     pieces, ends = [], []
     for c in range(3):
         turned = speeds[c].T
@@ -382,6 +384,7 @@
     for i in range(6, 8):
         trade(i).start()
     place_rows(gz, high_part, low_hot, jnp.concatenate(thirds(values), 0), second, parcel_rows)
+    pass_on(2)
     turned = jnp.concatenate(pieces[2:], 0)
     turned_axial = jnp.concatenate(pieces[:2], 0)
     fluid[...] = jnp.zeros_like(fluid)
@@ -395,11 +398,12 @@
         deposit_slab(peer(o), first_in, turned, fluid, deposit, (1, 2))
 
     done = 1
-    for i in range(6):
-        upto = 1 + (i + 1) * (gz - 1) // 6
+    for i in range(3, 6):
+        pass_on(i)
+        upto = min(gz, done + 1 + gz // 8)
         loop(done, upto, take)
         done = upto
-        pass_on(i)
+    loop(done, gz, take)
     for c in sides:
         c.wait()
     for c in loads[5:]:
@@ -409,6 +413,7 @@
     for c in (1, 2):
         ustar[c] = most_of(c, speeds, near, edge_l, edge_r, deposit, weights)
     far_ready(range(6))
+    loop(1, gz, lambda o: second_copy(gz - o).start())
     radial, azimuthal = [ustar[c] + far_part(c, speeds, nu, far) for c in (1, 2)]
     ustar[1] = radial
     ustar[2] = azimuthal
@@ -436,7 +441,6 @@
         outer[-1].start()
     for i in (6, 7):
         pass_on(i)
-    loop(1, gz, lambda o: second_copy(gz - o).start())
 
     def axial(o):
         deposit_slab(peer(o), first_in, turned_axial, fluid, deposit, (0,))

time: 34.1 us -> 34.3 us (level)
  no operation moved by 1% of the time
where the time goes in v7:
time: 34.3 us; the launch traced here: 33.8 us
  Pallas kernels  32.5 us (95%)
  between operations  1.29 us (4%)
    pallas_call x1, Pallas kernels, body(): pl.pallas_call(functools.partial(main_kernel, gz, pa), out_shape=(shape(3...  29.9 us
    pallas_call x1, Pallas kernels, body(): pl.pallas_call(functools.partial(finish_kernel, gz, pa, flat), out_shape=...  2.62 us

profile of v7, /device:TPU:1, one launch (start us, length us, event | category | flops | bytes accessed | tf_op | source)
XLA Modules:
  0.0 33.8 jit_solution(42256062734843618)
XLA Ops:
  1.3 29.9 %step.1 = (f32[3,192,128]{2,1,0:T(8,128)}, f32[4,192,128]{2,1,0:T(8,128)}, f32[8,16,384]{2,1,0:T(8,128)}, f32[8,8,384]{2,1,0:T(8,128)}) custom-call(s32[1]{0:T(128)S(6)} %copy.14.counts, s32[1,1024]{1,0:T(1,128)} %bitcast.11, s32[1,1024]{1,0:T(1,128)} %bitcast.12, f32[16,1024]{1,0:T(8,128)} %bitcast.10, f32[3,192,128]{2,1,0:T(8,128)} %bitcast.9, ...), custom_call_target="tpu_custom_call" | custom-call | tf_op jit(solution)/shard_map/step/pallas_call | solution.py:550
  31.1 2.6 %finish.1 = (f32[3,192,128]{2,1,0:T(8,128)}, f32[16,3072]{1,0:T(8,128)}) custom-call(s32[1]{0:T(128)} %bitcast.where, f32[4,192,128]{2,1,0:T(8,128)} %get-tuple-element.8.hat, f32[3,192,128]{2,1,0:T(8,128)} %get-tuple-element.9.ustar, bf16[4,2,512,128]{3,2,1,0:T(8,128)(2,1)} %constant.17.clone.high, bf16[4,2,512,128]{3,2,1,0:T(8,128)(2,1)} %constant.18.clone.low, ...), custom_call_target="tpu_custom_call" | custom-call | tf_op jit(solution)/shard_map/finish/pallas_call | solution.py:572

commit v8 on v7

--- a/solution.py
+++ b/solution.py
@@ -413,7 +413,6 @@
     for c in (1, 2):
         ustar[c] = most_of(c, speeds, near, edge_l, edge_r, deposit, weights)
     far_ready(range(6))
-    loop(1, gz, lambda o: second_copy(gz - o).start())
     radial, azimuthal = [ustar[c] + far_part(c, speeds, nu, far) for c in (1, 2)]
     ustar[1] = radial
     ustar[2] = azimuthal
@@ -441,6 +440,7 @@
         outer[-1].start()
     for i in (6, 7):
         pass_on(i)
+    loop(1, gz, lambda o: second_copy(gz - o).start())
 
     def axial(o):
         deposit_slab(peer(o), first_in, turned_axial, fluid, deposit, (0,))

time: 34.3 us -> 34.3 us (level)
  no operation moved by 1% of the time
where the time goes in v8:
time: 34.3 us; the launch traced here: 33.7 us
  Pallas kernels  32.5 us (95%)
  between operations  1.29 us (4%)
    pallas_call x1, Pallas kernels, body(): pl.pallas_call(functools.partial(main_kernel, gz, pa), out_shape=(shape(3...  29.8 us
    pallas_call x1, Pallas kernels, body(): pl.pallas_call(functools.partial(finish_kernel, gz, pa, flat), out_shape=...  2.62 us

profile of v8, /device:TPU:1, one launch (start us, length us, event | category | flops | bytes accessed | tf_op | source)
XLA Modules:
  0.0 33.7 jit_solution(4148428472326705293)
XLA Ops:
  1.3 29.8 %step.1 = (f32[3,192,128]{2,1,0:T(8,128)}, f32[4,192,128]{2,1,0:T(8,128)}, f32[8,16,384]{2,1,0:T(8,128)}, f32[8,8,384]{2,1,0:T(8,128)}) custom-call(s32[1]{0:T(128)S(6)} %copy.14.counts, s32[1,1024]{1,0:T(1,128)} %bitcast.11, s32[1,1024]{1,0:T(1,128)} %bitcast.12, f32[16,1024]{1,0:T(8,128)} %bitcast.10, f32[3,192,128]{2,1,0:T(8,128)} %bitcast.9, ...), custom_call_target="tpu_custom_call" | custom-call | tf_op jit(solution)/shard_map/step/pallas_call | solution.py:550
  31.1 2.6 %finish.1 = (f32[3,192,128]{2,1,0:T(8,128)}, f32[16,3072]{1,0:T(8,128)}) custom-call(s32[1]{0:T(128)} %bitcast.where, f32[4,192,128]{2,1,0:T(8,128)} %get-tuple-element.8.hat, f32[3,192,128]{2,1,0:T(8,128)} %get-tuple-element.9.ustar, bf16[4,2,512,128]{3,2,1,0:T(8,128)(2,1)} %constant.17.clone.high, bf16[4,2,512,128]{3,2,1,0:T(8,128)(2,1)} %constant.18.clone.low, ...), custom_call_target="tpu_custom_call" | custom-call | tf_op jit(solution)/shard_map/finish/pallas_call | solution.py:572
